TPU v7x, 512 devices: a whole 4x4x16 slice. The times are simulated.
512 devices in a mesh: ctx: 16 (over x, y), exp: 32 (over z, core).
Axes of the slice: x: 4, y: 4, z: 16, core: 2. Of those that a mesh axis runs over, the one named last changes fastest.
Arguments:
- residual: bfloat16 [32, 2048, 2048], P('exp', 'ctx'), may hold values from -12 to 12
- queries: bfloat16 [32, 2048, 1536], P('exp', 'ctx'), may hold values from -8 to 8
- latent: bfloat16 [32, 2048, 576], P('exp', 'ctx'), may hold values from -8 to 8
- key_up: bfloat16 [512, 1024], replicated, may hold values from -0.5 to 0.5
- value_up: bfloat16 [512, 1024], replicated, may hold values from -0.25 to 0.25
- out_proj: bfloat16 [1024, 2048], P(None, 'ctx'), may hold values from -0.1875 to 0.1875
- norm_gain: float32 [2048], replicated, may hold values from 0.4 to 2.5
- w_gate: bfloat16 [32, 2048, 704], P('exp', None, 'ctx'), may hold values from -0.125 to 0.125
- w_up: bfloat16 [32, 2048, 704], P('exp', None, 'ctx'), may hold values from -0.125 to 0.125
- w_down: bfloat16 [32, 704, 2048], P('exp', 'ctx'), may hold values from -0.21875 to 0.21875
- routes: int32 [32, 2048, 2], P('exp', 'ctx'), may hold values from 0 to 31, all different within a row; in each aligned block of 128 rows (0 to 127, 128 to 255, ..., all dimensions but the last counted through in order) at most 9 rows name the same one
- route_weights: float32 [32, 2048, 2], P('exp', 'ctx'), may hold values from 0.2 to 1
Outputs:
- layer_out: bfloat16 [32, 2048, 2048], P('exp', 'ctx')
Inputs may be any that keep to these rules, and one draw needn't show every extreme that they name: `routes`: the 2 experts of a token differ; among the 128 tokens of one device (aligned blocks of the sequences laid end to end) no expert is named more than 9 times, a bound that some block reaches.
All inputs are finite; a program needn't handle non-finite values.
Results may differ from a plain program's by a relative error of at most 0.022.
Values may be sent and summed in bfloat16 or wider, within the bound.
No kernel may reach another device: no remote copies, remote signals or barrier semaphores. Data moves between devices by JAX's collectives and lax.ppermute only.
A program may use at most 128 MiB of HBM per device.

v0:
```python
import jax
import jax.numpy as jnp
from jax import lax
from jax.sharding import PartitionSpec as P

D = 2048
HEADS = 8
NOPE = 128
ROPE = 64
VHEAD = 128
LATENT = 512
EXP_DEV = 1
TOPK = 2


def fetch_experts(w_gate, w_up, w_down):
    return (
        lax.all_gather(w_gate[0], "ctx", axis=1, tiled=True),
        lax.all_gather(w_up[0], "ctx", axis=1, tiled=True),
        lax.all_gather(w_down[0], "ctx", axis=0, tiled=True),
    )


def body(
    residual,
    queries,
    latent,
    key_up,
    value_up,
    out_proj,
    norm_gain,
    w_gate,
    w_up,
    w_down,
    routes,
    route_weights,
):
    tok_rows = residual.shape[1]
    ctx_index = lax.axis_index("ctx")
    query_rows = queries[0]
    groups = [(0, tok_rows, ctx_index * tok_rows + jnp.arange(tok_rows, dtype=jnp.int32))]
    query_heads = query_rows.reshape(tok_rows, HEADS, NOPE + ROPE)
    key_heads = key_up.reshape(LATENT, HEADS, NOPE)
    absorbed = jnp.einsum(
        "thn,lhn->thl", query_heads[:, :, :NOPE], key_heads, preferred_element_type=jnp.float32
    ).astype(jnp.bfloat16)
    query_rope = query_heads[:, :, NOPE:]
    score_scale = (NOPE + ROPE) ** (-0.5)
    initial = tuple(
        (
            (
                jnp.full((HEADS, stop - start), -1e30, jnp.float32),
                jnp.zeros((HEADS, stop - start), jnp.float32),
                jnp.zeros((stop - start, HEADS, LATENT), jnp.float32),
            )
            for start, stop, query_pos in groups
        )
    )
    offset = jnp.int32(0)
    key_rows = lax.all_gather(latent, "ctx", axis=1, tiled=True)[0]
    row_count = key_rows.shape[0]
    key_pos = jnp.arange(row_count, dtype=jnp.int32)
    results = []
    for group, state_in in zip(groups, initial):
        start, stop, query_pos = group

        def update(state):
            running, denominator, numerator = state
            scores = jnp.einsum(
                "thl,sl->hts", absorbed, key_rows[:, :LATENT], preferred_element_type=jnp.float32
            )
            scores = scores + jnp.einsum(
                "thr,sr->hts", query_rope, key_rows[:, LATENT:], preferred_element_type=jnp.float32
            )
            scores = scores * score_scale
            scores = jnp.where(key_pos[None, None, :] <= query_pos[None, :, None], scores, -1e30)
            updated = jnp.maximum(running, jnp.max(scores, axis=-1))
            factor = jnp.exp(running - updated)
            expo = jnp.exp(scores - updated[:, :, None])
            denominator = jnp.sum(expo, axis=-1)
            added = jnp.einsum(
                "hts,sl->thl",
                expo.astype(jnp.bfloat16),
                key_rows[:, :LATENT],
                preferred_element_type=jnp.float32,
            )
            numerator = numerator * factor.T[:, :, None] + added
            return (updated, denominator, numerator)

        def keep_state(state):
            return state

        results.append(lax.cond(offset <= query_pos[-1], update, keep_state, state_in))
    final_states = tuple(results)
    context = jnp.concatenate(
        [
            (numerator / denominator.T[:, :, None]).astype(jnp.bfloat16)
            for running, denominator, numerator in final_states
        ],
        axis=0,
    )
    value_heads = value_up.reshape(LATENT, HEADS, VHEAD)
    flat_values = jnp.einsum(
        "thl,lhv->thv", context, value_heads, preferred_element_type=jnp.float32
    ).astype(jnp.bfloat16)
    flat_values = flat_values.reshape(tok_rows, HEADS * VHEAD)
    projected = jnp.dot(
        flat_values,
        lax.all_gather(out_proj, "ctx", axis=1, tiled=True),
        preferred_element_type=jnp.float32,
    )
    attended = (residual[0].astype(jnp.float32) + projected).astype(jnp.bfloat16)
    wide = attended.astype(jnp.float32)
    scale_rows = lax.rsqrt(jnp.mean(wide * wide, axis=-1, keepdims=True) + 1e-06)
    normed = (wide * scale_rows * norm_gain).astype(jnp.bfloat16)
    gathered = fetch_experts(w_gate, w_up, w_down)
    gate_full, up_full, down_full = gathered
    experts = lax.axis_size("exp") * EXP_DEV
    capacity = max(2, tok_rows * TOPK * 9 // (8 * experts))
    pairs = tok_rows * TOPK
    flat_routes = routes[0].reshape(pairs)
    onehot = (flat_routes[:, None] == jnp.arange(experts, dtype=jnp.int32)[None, :]).astype(
        jnp.int32
    )
    earlier = jnp.cumsum(onehot, axis=0) - onehot
    position = jnp.sum(earlier * onehot, axis=1)
    slot_index = flat_routes * capacity + position
    token_of = jnp.arange(pairs, dtype=jnp.int32) // TOPK
    outgoing = jnp.zeros((experts * capacity, D), jnp.bfloat16).at[slot_index].set(normed[token_of])
    outgoing = outgoing.reshape(experts, capacity, D)
    slot_rows = lax.all_to_all(outgoing, "exp", split_axis=0, concat_axis=0, tiled=True)
    sources = slot_rows.shape[0]
    row_count = slot_rows.shape[1]
    flat_rows = slot_rows.reshape(sources * row_count, D)
    gate_proj = jnp.dot(flat_rows, gate_full, preferred_element_type=jnp.float32)
    up_proj = jnp.dot(flat_rows, up_full, preferred_element_type=jnp.float32)
    activation = (jax.nn.silu(gate_proj) * up_proj).astype(jnp.bfloat16)
    result = jnp.dot(activation, down_full, preferred_element_type=jnp.float32).astype(jnp.bfloat16)
    result = result.reshape(sources, row_count, D)
    returned = lax.all_to_all(result, "exp", split_axis=0, concat_axis=0, tiled=True)
    picked = returned.reshape(experts * capacity, D)[slot_index].astype(jnp.float32)
    picked = picked.reshape(tok_rows, TOPK, D)
    mixed = jnp.sum(picked * route_weights[0][:, :, None], axis=1)
    layer_out = (wide + mixed).astype(jnp.bfloat16)
    return layer_out[None]


def solution(mesh):
    return jax.shard_map(
        body,
        mesh=mesh,
        in_specs=(
            P("exp", "ctx", None),
            P("exp", "ctx", None),
            P("exp", "ctx", None),
            P(),
            P(),
            P(None, "ctx"),
            P(),
            P("exp", None, "ctx"),
            P("exp", None, "ctx"),
            P("exp", "ctx", None),
            P("exp", "ctx", None),
            P("exp", "ctx", None),
        ),
        out_specs=P("exp", "ctx", None),
        check_vma=False,
    )
```

profile of v0, /device:TPU:1, one launch (start us, length us, event | category | flops | bytes accessed | tf_op | source)
XLA Modules:
  0.0 527.5 jit_solution(2107951873388162743)
XLA Ops:
  6.6 1.9 copy.52
  8.5 0.7 all-gather.11.cloned.1.call-update
  9.3 2.0 copy.62
  11.3 1.9 copy.63
  13.3 1.0 copy.64
  16.3 1.4 copy.70
  18.8 1.5 fusion.23
  20.4 56.7 %all-gather.9.cloned.1.call-done = bf16[1,2048,576]{2,1,0:T(8,128)(2,1)} async-done(((bf16[1,128,576]{2,1,0:T(8,128)(2,1)}), bf16[1,2048,576]{2,1,0:T(8,128)(2,1)}) %all-gather.9.cloned.1.call-update) | async-done | bytes 2359312 | tf_op jit(solution)/shard_map/all_gather | solution.py:60
  77.0 10.3 %conditional.1 = (f32[8,128]{1,0:T(8,128)S(1)}, f32[128,8,512]{2,0,1:T(8,128)S(1)}) conditional(s32[]{:T(128)} %bitcast.7, () %tuple.13, (s32[2048]{0:T(1024)S(1)}, s32[128]{0:T(128)S(1)}, bf16[1,2048,576]{2,1,0:T(8,128)(2,1)}, bf16[128,8,512]{0,2,1:T(8,128)(2,1)}, bf16[128,8,192]{0,2,1:T(8,128)(2,1)S(1)}) %tuple.34), branch_computations={%region_0.0_spmd, %region_1.4_spmd} | conditional | flops 4580967424 | bytes 59941420 | solution.py:93
  77.0 4.3 fusion.7
  81.7 1.9 fusion.45
  83.6 2.4 bitcast_add_fusion
  86.1 1.1 fusion.1
  87.4 1.8 convolution_convert_fusion.1
  89.2 62.6 %all-gather.11.cloned.1.call-done = bf16[1024,2048]{1,0:T(8,128)(2,1)} async-done(((bf16[1024,128]{1,0:T(8,128)(2,1)}), bf16[1024,2048]{1,0:T(8,128)(2,1)}) %all-gather.11.cloned.1.call-update) | async-done | bytes 4194320 | tf_op jit(solution)/shard_map/all_gather | solution.py:109
  151.8 3.0 multiply_reduce_fusion.1
  155.0 5.8 %scatter_custom_fusion = bf16[288,2048]{1,0:T(8,128)(2,1)S(1)} fusion(s32[256]{0:T(256)S(1)} %bitcast.90, bf16[128,2048]{1,0:T(8,128)(2,1)S(1)} %multiply_convert_fusion, s32[1024]{0:T(1024)S(1)} %pad_clamp_fusion.1, bf16[]{:T(256)} %constant.52.clone.1), kind=kCustom, calls=%fused_computation.39 | custom fusion | bytes 1179650 | tf_op jit(solution)/shard_map/scatter | solution.py:129
  160.8 1.6 reshape.170
  162.4 114.6 %all_to_all.10 = bf16[32,9,2048]{2,1,0:T(8,128)(2,1)} all-to-all(bf16[32,9,2048]{2,1,0:T(8,128)(2,1)} %reshape.170), channel_id=1, replica_groups=mesh['ctx'=16,'exp'=32] {'exp'}, dimensions={0} | all-to-all | bytes 2359296 | tf_op jit(solution)/shard_map/all_to_all | solution.py:131
  277.1 1.8 reshape.171
  278.9 6.2 %fusion.15 = f32[288,704]{1,0:T(8,128)} fusion(bf16[288,2048]{1,0:T(8,128)(2,1)S(1)} %reshape.171, bf16[1,2048,704]{1,0,2:T(2,128)(2,1)} %all-gather.13.cloned.1.call-done), kind=kOutput, calls=%fused_computation.23 | convolution fusion | flops 830472192 | bytes 4874240 | tf_op jit(solution)/shard_map/dot_general | solution.py:135
  285.1 21.1 %all-gather.15.cloned.1.call-done = bf16[1,2048,704]{1,0,2:T(2,128)(2,1)} async-done(((bf16[1,2048,44]{1,0,2:T(2,128)(2,1)}), bf16[1,2048,704]{1,0,2:T(2,128)(2,1)}) %all-gather.15.cloned.1.call-update) | async-done | bytes 2883600 | tf_op jit(solution)/shard_map/all_gather | solution.py:19
  306.1 76.9 %all-gather.17.cloned.1.call-done = bf16[1,704,2048]{2,0,1:T(2,128)(2,1)} async-done(((bf16[1,44,2048]{2,0,1:T(2,128)(2,1)}), bf16[1,704,2048]{2,0,1:T(2,128)(2,1)}) %all-gather.17.cloned.1.call-update) | async-done | bytes 2883600 | tf_op jit(solution)/shard_map/all_gather | solution.py:20
  383.0 9.6 %fusion.18 = bf16[288,2048]{1,0:T(8,128)(2,1)} fusion(bf16[1,704,2048]{2,0,1:T(2,128)(2,1)} %all-gather.17.cloned.1.call-done, bf16[288,2048]{1,0:T(8,128)(2,1)S(1)} %reshape.171, bf16[1,2048,704]{1,0,2:T(2,128)(2,1)} %all-gather.15.cloned.1.call-done, f32[288,704]{1,0:T(8,128)} %fusion.15), kind=kOutput, calls=%fused_computation.26 | convolution fusion | flops 1662750720 | bytes 8937472 | tf_op jit(solution)/shard_map/dot_general | solution.py:138
  392.7 2.7 reshape.172
  395.3 13.2 %all-to-all-start.1 = ((bf16[32,9,2048]{2,1,0:T(8,128)(2,1)}), bf16[32,9,2048]{2,1,0:T(8,128)(2,1)}, u32[]{:S(2)}, u32[]{:S(2)}) async-start(bf16[32,9,2048]{2,1,0:T(8,128)(2,1)} %reshape.172), calls=%async_computation.1 | async-start | bytes 4194304 | tf_op jit(solution)/shard_map/all_to_all | solution.py:140
  408.7 98.9 %all-to-all-done.1 = bf16[32,9,2048]{2,1,0:T(8,128)(2,1)} async-done(((bf16[32,9,2048]{2,1,0:T(8,128)(2,1)}), bf16[32,9,2048]{2,1,0:T(8,128)(2,1)}, u32[]{:S(2)}, u32[]{:S(2)}) %all-to-all-start.1) | async-done | bytes 1179680 | tf_op jit(solution)/shard_map/all_to_all | solution.py:140
  507.6 1.8 reshape.173
  509.4 2.4 gather_fusion
  511.7 3.5 reshape.176
  515.2 4.8 multiply_reduce_fusion
  520.0 0.9 fusion.37
  (55 shorter events, 3.4 us)
Async XLA Ops:
  6.5 12.2 %copy-start = (bf16[512,1024]{1,0:T(8,128)(2,1)S(1)}, bf16[512,1024]{1,0:T(8,128)(2,1)}, u32[]{:S(2)}) copy-start(bf16[512,1024]{1,0:T(8,128)(2,1)} %param.17) | copy-start | bytes 3145732
  6.5 6.8 %copy-start.6 = (bf16[1,44,2048]{2,1,0:T(8,128)(2,1)S(1)}, bf16[1,44,2048]{2,1,0:T(8,128)(2,1)}, u32[]{:S(2)}) copy-start(bf16[1,44,2048]{2,1,0:T(8,128)(2,1)} %param.23) | copy-start | bytes 540676
  6.5 7.8 %copy-start.8 = (s32[1,128,2]{1,2,0:T(2,128)S(1)}, s32[1,128,2]{1,2,0:T(2,128)}, u32[]{:S(2)}) copy-start(s32[1,128,2]{1,2,0:T(2,128)} %param.24) | copy-start | bytes 3076
  6.5 8.3 %copy-start.5 = (bf16[1,128,1536]{2,1,0:T(8,128)(2,1)S(1)}, bf16[1,128,1536]{2,1,0:T(8,128)(2,1)}, u32[]{:S(2)}) copy-start(bf16[1,128,1536]{2,1,0:T(8,128)(2,1)} %param.15) | copy-start | bytes 1179652
  6.5 9.7 %copy-start.3 = (bf16[512,1024]{1,0:T(8,128)(2,1)S(1)}, bf16[512,1024]{1,0:T(8,128)(2,1)}, u32[]{:S(2)}) copy-start(bf16[512,1024]{1,0:T(8,128)(2,1)} %param.18) | copy-start | bytes 3145732
  6.5 70.5 %all-gather.9.cloned.1.call-start = ((), (), s32[]{:S(2)}) async-start(), calls=%async_computation.2 | async-start | bytes 2785280 | tf_op jit(solution)/shard_map/all_gather | solution.py:60
  8.5 143.3 %all-gather.11.cloned.1.call-start = ((), (), s32[]{:S(2)}) async-start(), calls=%async_computation.3 | async-start | bytes 4456448 | tf_op jit(solution)/shard_map/all_gather | solution.py:109
  9.2 269.7 %all-gather.13.cloned.1.call-start = ((), (), s32[]{:S(2)}) async-start(), calls=%async_computation.4 | async-start | bytes 6127616 | tf_op jit(solution)/shard_map/all_gather | solution.py:18
  11.3 294.9 %all-gather.15.cloned.1.call-start = ((), (), s32[]{:S(2)}) async-start(), calls=%async_computation.5 | async-start | bytes 6127616 | tf_op jit(solution)/shard_map/all_gather | solution.py:19
  13.3 369.8 %all-gather.17.cloned.1.call-start = ((), (), s32[]{:S(2)}) async-start(), calls=%async_computation.6 | async-start | bytes 6127616 | tf_op jit(solution)/shard_map/all_gather | solution.py:20
  77.0 4.7 copy-start.2
  87.4 64.5 %copy-start.4 = (bf16[1,128,2048]{2,1,0:T(8,128)(2,1)S(1)}, bf16[1,128,2048]{2,1,0:T(8,128)(2,1)}, u32[]{:S(2)}) copy-start(bf16[1,128,2048]{2,1,0:T(8,128)(2,1)} %param.14) | copy-start | bytes 1572868
  151.8 3.0 copy-start.7
  395.3 13.2 %copy-start.9 = (f32[1,128,2]{1,2,0:T(2,128)S(1)}, f32[1,128,2]{1,2,0:T(2,128)}, u32[]{:S(2)}) copy-start(f32[1,128,2]{1,2,0:T(2,128)} %param.25) | copy-start | bytes 3076
  395.3 112.2 %all-to-all-start.1 = ((bf16[32,9,2048]{2,1,0:T(8,128)(2,1)}), bf16[32,9,2048]{2,1,0:T(8,128)(2,1)}, u32[]{:S(2)}, u32[]{:S(2)}) async-start(bf16[32,9,2048]{2,1,0:T(8,128)(2,1)} %reshape.172), calls=%async_computation.1 | async-start | bytes 4194304 | tf_op jit(solution)/shard_map/all_to_all | solution.py:140
  511.7 9.3 %copy-start.1 = (bf16[512,1024]{1,0:T(8,128)(2,1)S(1)}, bf16[512,1024]{1,0:T(8,128)(2,1)}, u32[]{:S(2)}) copy-start(bf16[512,1024]{1,0:T(8,128)(2,1)} %param.17) | copy-start | bytes 3145732
Sparse Core Ops, SparseCore 0:
  10.4 66.5 all-gather.8
  80.0 71.7 all-gather.10
  154.9 74.4 all-gather.12
  232.3 73.8 all-gather.14
  309.0 73.9 all-gather.16
where the time goes:
time: 528 us
  waiting for transfers between devices  317 us (60%)
  blocking collectives  115 us (22%)
  matrix products  30.7 us (6%)
  local copies, waits for them, and re-layouts  29.5 us (6%)
  between operations  14 us (3%)
  starting transfers between devices  13.4 us (3%)
  other arithmetic  8.13 us (2%)
    all_to_all x1, blocking collectives, body(): lax.all_to_all(outgoing, 'exp', split_axis=0, concat_axis=0, tiled=True)  115 us
    all_to_all x1, waiting for transfers between devices, body(): lax.all_to_all(result, 'exp', split_axis=0, concat_axis=0, tiled=True)  98.9 us
    all_gather x1, waiting for transfers between devices, fetch_experts(): lax.all_gather(w_down[0], 'ctx', axis=0, tiled=True)  76.9 us
    all_gather x1, waiting for transfers between devices, body(): lax.all_gather(out_proj, 'ctx', axis=1, tiled=True)  62.6 us
    all_gather x1, waiting for transfers between devices, body(): key_rows = lax.all_gather(latent, 'ctx', axis=1, tiled=True)[0]  56.7 us
    all_gather x1, waiting for transfers between devices, fetch_experts(): lax.all_gather(w_up[0], 'ctx', axis=1, tiled=True)  21.1 us
    all_to_all x1, starting transfers between devices, body(): lax.all_to_all(result, 'exp', split_axis=0, concat_axis=0, tiled=True)  13.2 us
  transfers between devices with their start and end apart: 6, of which 5 were waited for; matrix products, arithmetic and copies ran while one was open for 8% of the time, Pallas kernels for 0%

commit v1 on v0

v1 whole, which is shorter than its diff:
```python
import jax
import jax.numpy as jnp
from jax import lax
from jax.experimental import pallas as pl
from jax.experimental.pallas import tpu as pltpu
from jax.sharding import PartitionSpec as P

D = 2048
HEADS = 8
NOPE = 128
ROPE = 64
QK = NOPE + ROPE
VHEAD = 128
LATENT = 512
FF_DEV = 44
FF_PAD = 48
CAP = 9
LANES = 128
F32 = jnp.float32
BF16 = jnp.bfloat16
NT = (((1,), (1,)), ((), ()))
TN = (((0,), (0,)), ((), ()))
VMEM_LIMIT = 60 << 20


def call(kernel, out_shape, scratch=(), flops=0, moved=0, in_specs=None):
    options = {} if in_specs is None else {"in_specs": in_specs}
    return pl.pallas_call(
        kernel,
        out_shape=out_shape,
        scratch_shapes=list(scratch),
        compiler_params=pltpu.CompilerParams(vmem_limit_bytes=VMEM_LIMIT),
        cost_estimate=pl.CostEstimate(flops=flops, bytes_accessed=moved, transcendentals=0),
        **options,
    )


def vmem():
    return pl.BlockSpec(memory_space=pltpu.VMEM)


def slot_matrix(slots, k, rows):
    return lax.broadcasted_iota(jnp.int32, (rows, slots.shape[1]), 0) == slots[k : k + 1, :]


def fill_rows(matrix, source_ref, scratch, out_ref):
    rows = matrix.shape[0]
    parts = source_ref.shape[1] // LANES
    for j in range(0, parts, 2):
        chunk = jnp.dot(matrix, source_ref[:, j * LANES : (j + 2) * LANES], preferred_element_type=F32)
        scratch[pl.ds(j, rows, stride=parts), :] = chunk[:, :LANES]
        scratch[pl.ds(j + 1, rows, stride=parts), :] = chunk[:, LANES:]
    out_ref[...] = scratch[...].astype(BF16)


def pack_latent(latent_ref, out_ref):
    tokens = latent_ref.shape[0]
    half = tokens // 2
    for c in range(out_ref.shape[0]):
        for j in range(LATENT // LANES):
            out_ref[c, j * tokens : (j + 1) * tokens, :] = latent_ref[:, j * LANES : (j + 1) * LANES]
        start = LATENT // LANES * tokens
        rope = latent_ref[:, LATENT:]
        out_ref[c, start : start + half, :] = jnp.concatenate([rope[:half], rope[half:]], axis=1)


def dispatch_residual(routes_ref, residual_ref, out_ref, slots_ref, scratch):
    tokens = routes_ref.shape[1]
    rows = scratch.shape[0] * LANES // D
    expert = lax.broadcasted_iota(jnp.int32, (LANES, tokens), 0)
    first = (expert == routes_ref[0:1, :]).astype(F32)
    second = (expert == routes_ref[1:2, :]).astype(F32)
    row = lax.broadcasted_iota(jnp.int32, (tokens, tokens), 0)
    column = lax.broadcasted_iota(jnp.int32, (tokens, tokens), 1)
    before = (row < column).astype(BF16)
    count_first = jnp.dot(first.astype(BF16), before, preferred_element_type=F32)
    count_second = jnp.dot(second.astype(BF16), before, preferred_element_type=F32)
    count_second = count_second + jnp.sum(first, axis=1, keepdims=True)
    place_first = jnp.sum(count_first * first, axis=0, keepdims=True).astype(jnp.int32)
    place_second = jnp.sum(count_second * second, axis=0, keepdims=True).astype(jnp.int32)
    slots = jnp.concatenate(
        [routes_ref[0:1, :] * CAP + place_first, routes_ref[1:2, :] * CAP + place_second], axis=0
    )
    slots_ref[...] = slots
    matrix = (slot_matrix(slots, 0, rows) | slot_matrix(slots, 1, rows)).astype(BF16)
    fill_rows(matrix, residual_ref, scratch, out_ref)


def absorb(queries_ref, key_up_ref, out_ref):
    tokens = queries_ref.shape[0]
    for h in range(HEADS):
        query = queries_ref[:, h * QK : (h + 1) * QK]
        keys = key_up_ref[:, h * NOPE : (h + 1) * NOPE]
        out_ref[h * tokens : (h + 1) * tokens, :LATENT] = lax.dot_general(
            query[:, :NOPE], keys, NT, preferred_element_type=F32
        ).astype(BF16)
        out_ref[h * tokens : (h + 1) * tokens, LATENT:] = query[:, NOPE:]


def attend(place_ref, slots_ref, latent_ref, absorbed_ref, value_up_ref, values_ref, out_ref, keys, scratch):
    tokens = values_ref.shape[0]
    half = tokens // 2
    for c in range(latent_ref.shape[0]):
        for j in range(LATENT // LANES):
            keys[c * tokens : (c + 1) * tokens, j * LANES : (j + 1) * LANES] = latent_ref[
                c, j * tokens : (j + 1) * tokens, :
            ]
        rope = latent_ref[c, LATENT // LANES * tokens : LATENT // LANES * tokens + half, :]
        keys[c * tokens : c * tokens + half, LATENT:] = rope[:, :ROPE]
        keys[c * tokens + half : (c + 1) * tokens, LATENT:] = rope[:, ROPE:]
    span = keys.shape[0]
    group = 2 * tokens
    query_at = lax.broadcasted_iota(jnp.int32, (group, 1), 0) % tokens + place_ref[0] * tokens
    key_at = lax.broadcasted_iota(jnp.int32, (1, span), 1)
    allowed = key_at <= query_at
    for g in range(HEADS // 2):
        score = lax.dot_general(
            absorbed_ref[g * group : (g + 1) * group, :], keys[...], NT, preferred_element_type=F32
        )
        score = jnp.where(allowed, score * QK ** (-0.5), -1e30)
        highest = jnp.max(score, axis=1, keepdims=True)
        expo = jnp.exp(score - highest)
        denominator = jnp.sum(expo, axis=1, keepdims=True)
        context = jnp.dot(expo.astype(BF16), keys[:, :LATENT], preferred_element_type=F32)
        context = (context / denominator).astype(BF16)
        for i in range(2):
            h = 2 * g + i
            values_ref[:, h * VHEAD : (h + 1) * VHEAD] = jnp.dot(
                context[i * tokens : (i + 1) * tokens],
                value_up_ref[:, h * VHEAD : (h + 1) * VHEAD],
                preferred_element_type=F32,
            ).astype(BF16)
    rows = scratch.shape[0] * LANES // values_ref.shape[1]
    slots = slots_ref[...]
    matrix = (slot_matrix(slots, 0, rows) | slot_matrix(slots, 1, rows)).astype(BF16)
    fill_rows(matrix, values_ref, scratch, out_ref)


def lay_projection(parts, projection):
    depth = parts.shape[1]
    for c in range(parts.shape[0]):
        for j in range(parts.shape[2] // LANES):
            projection[j * depth : (j + 1) * depth, c * LANES : (c + 1) * LANES] = parts[
                c, :, j * LANES : (j + 1) * LANES
            ]


def take_rows(source_ref, scratch, parts, store):
    scratch[...] = source_ref[...].astype(F32)
    rows = scratch.shape[0] // parts
    for j in range(parts):
        store(j, scratch[pl.ds(j, rows, stride=parts), :])


def expert(
    residual_ref, values_ref, gain_ref, packed_ref, out_ref,
    parts, gate, up, down, projection, tall, short, values, wide, sems,
):
    depth = parts.shape[1]
    copies = []
    start = 0
    for n, buffer in enumerate((parts, gate, up, down)):
        size = buffer.shape[1]
        copies.append(pltpu.make_async_copy(packed_ref.at[:, start : start + size, :], buffer, sems.at[n]))
        copies[-1].start()
        start += size

    def keep_value(j, column):
        values[:, j * LANES : (j + 1) * LANES] = column.astype(BF16)

    def keep_wide(j, column):
        wide[:, j * LANES : (j + 1) * LANES] = column

    take_rows(values_ref, short, values.shape[1] // LANES, keep_value)
    take_rows(residual_ref, tall, D // LANES, keep_wide)
    copies[0].wait()
    lay_projection(parts, projection)
    attended = (wide[...] + jnp.dot(values[...], projection[...], preferred_element_type=F32)).astype(BF16)
    attended = attended.astype(F32)
    scale = lax.rsqrt(jnp.mean(attended * attended, axis=1, keepdims=True) + 1e-06)
    normed = (attended * scale * gain_ref[...]).astype(BF16)
    units = gate.shape[0] * gate.shape[1]
    copies[1].wait()
    gate_proj = lax.dot_general(normed, gate[...].reshape(units, D), NT, preferred_element_type=F32)
    copies[2].wait()
    up_proj = lax.dot_general(normed, up[...].reshape(units, D), NT, preferred_element_type=F32)
    activation = (gate_proj / (1.0 + jnp.exp(-gate_proj)) * up_proj).astype(BF16)
    copies[3].wait()
    rows = activation.shape[0]
    down_all = down[...].reshape(units, D)
    for j in range(0, D // LANES, 2):
        chunk = jnp.dot(activation, down_all[:, j * LANES : (j + 2) * LANES], preferred_element_type=F32)
        tall[pl.ds(j, rows, stride=D // LANES), :] = chunk[:, :LANES]
        tall[pl.ds(j + 1, rows, stride=D // LANES), :] = chunk[:, LANES:]
    out_ref[...] = tall[...].astype(BF16)


def home(residual_ref, values_ref, packed_ref, out_ref, parts, projection, sem):
    copy = pltpu.make_async_copy(packed_ref.at[:, : parts.shape[1], :], parts, sem)
    copy.start()
    copy.wait()
    lay_projection(parts, projection)
    projected = jnp.dot(values_ref[...], projection[...], preferred_element_type=F32)
    out_ref[...] = (residual_ref[...].astype(F32) + projected).astype(BF16)


def combine(slots_ref, weights_ref, attended_ref, rows_ref, out_ref, tall):
    slots = slots_ref[...]
    rows = tall.shape[0] * LANES // D
    first = slot_matrix(slots, 0, rows).astype(BF16)
    second = slot_matrix(slots, 1, rows).astype(BF16)
    weight_first = weights_ref[:, 0:1]
    weight_second = weights_ref[:, 1:2]

    def add(j, column):
        column = column.astype(BF16)
        picked_first = lax.dot_general(first, column, TN, preferred_element_type=F32)
        picked_second = lax.dot_general(second, column, TN, preferred_element_type=F32)
        mixed = picked_first * weight_first + picked_second * weight_second
        at = slice(j * LANES, (j + 1) * LANES)
        out_ref[:, at] = (attended_ref[:, at].astype(F32) + mixed).astype(BF16)

    take_rows(rows_ref, tall, D // LANES, add)


def body(
    residual, queries, latent, key_up, value_up, out_proj, norm_gain,
    w_gate, w_up, w_down, routes, route_weights,
):
    tokens = residual.shape[1]
    n_ctx = lax.axis_size("ctx")
    n_exp = lax.axis_size("exp")
    rows = n_exp * CAP
    flat = values_width = HEADS * VHEAD
    tall_rows = rows * D // LANES
    short_rows = rows * values_width // LANES
    block_rows = tokens * (LATENT + ROPE) // LANES

    latent_out = call(
        pack_latent, jax.ShapeDtypeStruct((n_ctx, block_rows, LANES), BF16), moved=3 << 20
    )(latent[0])
    latent_all = lax.all_to_all(latent_out, "ctx", split_axis=0, concat_axis=0, tiled=True)

    residual_out, slots = call(
        dispatch_residual,
        [jax.ShapeDtypeStruct((tall_rows, LANES), BF16), jax.ShapeDtypeStruct((2, tokens), jnp.int32)],
        scratch=[pltpu.VMEM((tall_rows, LANES), F32)],
        flops=2 * rows * tokens * D,
        moved=3 << 20,
    )(routes[0].T, residual[0])
    residual_rows = lax.all_to_all(
        residual_out.reshape(n_exp, tall_rows // n_exp, LANES), "exp", split_axis=0, concat_axis=0, tiled=True
    )

    pad = ((0, FF_PAD - w_gate.shape[2]), (0, 0))
    depth = flat // n_ctx
    packed = jnp.concatenate(
        [
            out_proj.reshape(n_ctx, depth, LANES).transpose(1, 0, 2).reshape(depth, n_ctx * LANES),
            jnp.pad(w_gate[0].T, pad),
            jnp.pad(w_up[0].T, pad),
            jnp.pad(w_down[0], pad),
        ],
        axis=0,
    )
    packed_all = lax.all_gather(packed, "ctx")

    absorbed = call(
        absorb,
        jax.ShapeDtypeStruct((HEADS * tokens, LATENT + ROPE), BF16),
        flops=2 * tokens * HEADS * NOPE * LATENT,
        moved=3 << 20,
    )(queries[0], key_up)
    place = lax.axis_index("ctx").astype(jnp.int32).reshape(1)
    values, values_out = call(
        attend,
        [
            jax.ShapeDtypeStruct((tokens, values_width), BF16),
            jax.ShapeDtypeStruct((short_rows, LANES), BF16),
        ],
        scratch=[
            pltpu.VMEM((n_ctx * tokens, LATENT + ROPE), BF16),
            pltpu.VMEM((short_rows, LANES), F32),
        ],
        flops=4 << 30,
        moved=6 << 20,
        in_specs=[pl.BlockSpec(memory_space=pltpu.SMEM)] + [vmem()] * 4,
    )(place, slots, latent_all, absorbed, value_up)
    values_rows = lax.all_to_all(
        values_out.reshape(n_exp, short_rows // n_exp, LANES), "exp", split_axis=0, concat_axis=0, tiled=True
    )

    weights_shape = (n_ctx, FF_PAD, D)
    result = call(
        expert,
        jax.ShapeDtypeStruct((tall_rows, LANES), BF16),
        scratch=[
            pltpu.VMEM((n_ctx, depth, D), BF16),
            pltpu.VMEM(weights_shape, BF16),
            pltpu.VMEM(weights_shape, BF16),
            pltpu.VMEM(weights_shape, BF16),
            pltpu.VMEM((values_width, D), BF16),
            pltpu.VMEM((tall_rows, LANES), F32),
            pltpu.VMEM((short_rows, LANES), F32),
            pltpu.VMEM((rows, values_width), BF16),
            pltpu.VMEM((rows, D), F32),
            pltpu.SemaphoreType.DMA((4,)),
        ],
        flops=4 << 30,
        moved=16 << 20,
        in_specs=[vmem()] * 3 + [pl.BlockSpec(memory_space=pl.ANY)],
    )(
        residual_rows.reshape(tall_rows, LANES),
        values_rows.reshape(short_rows, LANES),
        norm_gain.reshape(1, D),
        packed_all,
    )
    returned = lax.all_to_all(
        result.reshape(n_exp, tall_rows // n_exp, LANES), "exp", split_axis=0, concat_axis=0, tiled=True
    )

    attended = call(
        home,
        jax.ShapeDtypeStruct((tokens, D), BF16),
        scratch=[
            pltpu.VMEM((n_ctx, depth, D), BF16),
            pltpu.VMEM((values_width, D), BF16),
            pltpu.SemaphoreType.DMA,
        ],
        flops=2 * tokens * D * values_width,
        moved=6 << 20,
        in_specs=[vmem()] * 2 + [pl.BlockSpec(memory_space=pl.ANY)],
    )(residual[0], values, packed_all)
    layer_out = call(
        combine,
        jax.ShapeDtypeStruct((tokens, D), BF16),
        scratch=[pltpu.VMEM((tall_rows, LANES), F32)],
        flops=4 * rows * tokens * D,
        moved=3 << 20,
    )(slots, route_weights[0], attended, returned.reshape(tall_rows, LANES))
    return layer_out[None]


def solution(mesh):
    return jax.shard_map(
        body,
        mesh=mesh,
        in_specs=(
            P("exp", "ctx", None),
            P("exp", "ctx", None),
            P("exp", "ctx", None),
            P(),
            P(),
            P(None, "ctx"),
            P(),
            P("exp", None, "ctx"),
            P("exp", None, "ctx"),
            P("exp", "ctx", None),
            P("exp", "ctx", None),
            P("exp", "ctx", None),
        ),
        out_specs=P("exp", "ctx", None),
        check_vma=False,
    )
```

time: 528 us -> 285 us (0.54)
  waiting for transfers between devices: 317 us -> 80 us
  Pallas kernels: 0 us -> 42 us
  matrix products: 30.7 us -> 0 us
  local copies, waits for them, and re-layouts: 29.5 us -> 5.02 us
  blocking collectives: 115 us -> 129 us
  other arithmetic: 8.13 us -> 2.14 us
    all_gather x5 -> x1, waiting for transfers between devices: 217 us -> 0.01 us  [body(): packed_all = lax.all_gather(packed, 'ctx')]
    pallas_call x0 -> x7, Pallas kernels: none -> 42 us  [the longest x1 12.2 us: body(): call(attend, [jax.ShapeDtypeStruct((tokens, values_width), BF16), jax.Sha...]
    dot_general x8 -> x0, matrix products: 30.7 us -> none  [the longest x1 9.64 us: body(): jnp.dot(activation, down_full, preferred_element_type=jnp.float32)]
    all_to_all x1 -> x2, waiting for transfers between devices: 98.9 us -> 79.9 us  [the longest x1 54.8 us: body(): lax.all_to_all(result.reshape(n_exp, tall_rows // n_exp, LANES), 'exp', s...]
    all_to_all x1 -> x2, blocking collectives: 115 us -> 129 us  [the longest x1 65.4 us: body(): lax.all_to_all(residual_out.reshape(n_exp, tall_rows // n_exp, LANES), 'e...]
    reshape x5 -> x1, local copies, waits for them, and re-layouts: 9.27 us -> 1.03 us  [body(): out_proj.reshape(n_ctx, depth, LANES).transpose(1, 0, 2)]
    reduce_sum x3 -> x0, other arithmetic: 6.02 us -> none  [the longest x1 4.81 us: body(): mixed = jnp.sum(picked * route_weights[0][:, :, None], axis=1)]
    scatter x1 -> x0, local copies, waits for them, and re-layouts: 5.76 us -> none  [body(): jnp.zeros((experts * capacity, D), jnp.bfloat16).at[slot_index]]
  transfers between devices with their start and end apart: 6 -> 3, of which waited for: 5 -> 2; matrix products, arithmetic and copies ran while one was open for 8% -> 1% of each run, Pallas kernels for 0% -> 9%
where the time goes in v1:
time: 285 us; the launch traced here: 283 us
  blocking collectives  129 us (45%)
  waiting for transfers between devices  80 us (28%)
  Pallas kernels  42 us (15%)
  between operations  13.5 us (5%)
  starting transfers between devices  12.1 us (4%)
  local copies, waits for them, and re-layouts  5.02 us (2%)
    all_to_all x1, blocking collectives, body(): lax.all_to_all(residual_out.reshape(n_exp, tall_rows // n_exp, LANES), 'e...  65.4 us
    all_to_all x1, blocking collectives, body(): lax.all_to_all(values_out.reshape(n_exp, short_rows // n_exp, LANES), 'ex...  63.1 us
    all_to_all x1, waiting for transfers between devices, body(): lax.all_to_all(result.reshape(n_exp, tall_rows // n_exp, LANES), 'exp', s...  54.8 us
    all_to_all x1, waiting for transfers between devices, body(): lax.all_to_all(latent_out, 'ctx', split_axis=0, concat_axis=0, tiled=True)  25.1 us
    pallas_call x1, Pallas kernels, body(): call(attend, [jax.ShapeDtypeStruct((tokens, values_width), BF16), jax.Sha...  12.2 us
    pallas_call x1, Pallas kernels, body(): call(expert, jax.ShapeDtypeStruct((tall_rows, LANES), BF16), scratch=[plt...  11.2 us
    all_to_all x1, starting transfers between devices, body(): lax.all_to_all(latent_out, 'ctx', split_axis=0, concat_axis=0, tiled=True)  7.58 us
    pallas_call x1, Pallas kernels, body(): call(home, jax.ShapeDtypeStruct((tokens, D), BF16), scratch=[pltpu.VMEM((...  5.75 us
  transfers between devices with their start and end apart: 3, of which 2 were waited for; matrix products, arithmetic and copies ran while one was open for 1% of the time, Pallas kernels for 9%

profile of v1, /device:TPU:1, one launch (start us, length us, event | category | flops | bytes accessed | tf_op | source)
XLA Modules:
  0.0 283.2 jit_solution(6563432292849593141)
XLA Ops:
  6.5 0.0 copy-start.3
  6.5 0.0 all-gather.3.cloned.1.call-start
  6.5 1.0 copy.18
  7.6 2.1 fusion.6
  9.7 0.0 all-gather.3.cloned.1.call-update
  9.7 0.0 copy-done.3
  9.8 0.8 copy.14
  10.6 2.6 shard_map.119
  13.2 7.6 %all-to-all-start = ((bf16[16,576,128]{2,1,0:T(8,128)(2,1)}), bf16[16,576,128]{2,1,0:T(8,128)(2,1)S(1)}, u32[]{:S(2)}, u32[]{:S(2)}) async-start(bf16[16,576,128]{2,1,0:T(8,128)(2,1)} %shard_map.119), calls=%async_computation | async-start | bytes 4718592 | tf_op jit(solution)/shard_map/all_to_all | solution.py:242
  20.8 2.9 %shard_map.120.absorbed_ref = bf16[1024,576]{1,0:T(8,128)(2,1)} custom-call(bf16[128,1536]{1,0:T(8,128)(2,1)} %bitcast.43, bf16[512,1024]{1,0:T(8,128)(2,1)} %key_up_ref.1), custom_call_target="tpu_custom_call" | custom-call | flops 134217728 | bytes 3145728 | tf_op jit(solution)/shard_map/pallas_call | solution.py:268
  23.6 3.2 %shard_map.118 = (bf16[4608,128]{1,0:T(8,128)(2,1)}, s32[2,128]{1,0:T(2,128)}) custom-call(s32[2,128]{1,0:T(2,128)} %bitcast.50, bf16[128,2048]{1,0:T(8,128)(2,1)} %bitcast.41), custom_call_target="tpu_custom_call" | custom-call | flops 150994944 | bytes 3145728 | tf_op jit(solution)/shard_map/pallas_call | solution.py:244
  26.9 25.1 %all-to-all-done.latent_ref = bf16[16,576,128]{2,1,0:T(8,128)(2,1)S(1)} async-done(((bf16[16,576,128]{2,1,0:T(8,128)(2,1)}), bf16[16,576,128]{2,1,0:T(8,128)(2,1)S(1)}, u32[]{:S(2)}, u32[]{:S(2)}) %all-to-all-start) | async-done | bytes 2359328 | tf_op jit(solution)/shard_map/all_to_all | solution.py:242
  52.0 0.0 copy-start.1
  52.0 1.4 copy-done.1
  53.4 12.2 %shard_map.121 = (bf16[128,1024]{1,0:T(8,128)(2,1)}, bf16[2304,128]{1,0:T(8,128)(2,1)}) custom-call(s32[1]{0:T(128)} %bitcast.4.place_ref, s32[2,128]{1,0:T(2,128)} %get-tuple-element.9.slots_ref, bf16[16,576,128]{2,1,0:T(8,128)(2,1)} %copy-done.1, bf16[1024,576]{1,0:T(8,128)(2,1)} %shard_map.120.absorbed_ref, bf16[512,1024]{1,0:T(8,128)(2,1)} %value_up_ref.1), custom_call_target="tpu_custom_call" | custom-call | flops 4294967296 | bytes 6291456 | tf_op jit(solution)/shard_map/pallas_call | solution.py:275
  65.5 0.0 copy-start.2
  65.5 63.1 %all_to_all.20 = bf16[32,72,128]{2,1,0:T(8,128)(2,1)} all-to-all(bf16[32,72,128]{2,1,0:T(8,128)(2,1)} %bitcast.40), channel_id=1, replica_groups=mesh['ctx'=16,'exp'=32] {'exp'}, dimensions={0} | all-to-all | bytes 1179648 | tf_op jit(solution)/shard_map/all_to_all | solution.py:289
  128.7 0.0 copy-done.2
  128.7 65.4 %all_to_all.21 = bf16[32,144,128]{2,1,0:T(8,128)(2,1)} all-to-all(bf16[32,144,128]{2,1,0:T(8,128)(2,1)S(1)} %bitcast.37), channel_id=1, replica_groups=mesh['ctx'=16,'exp'=32] {'exp'}, dimensions={0} | all-to-all | bytes 2359296 | tf_op jit(solution)/shard_map/all_to_all | solution.py:251
  194.1 0.0 all-gather.3.cloned.1.call-done
  194.1 11.2 %shard_map.123 = bf16[4608,128]{1,0:T(8,128)(2,1)} custom-call(bf16[4608,128]{1,0:T(8,128)(2,1)} %bitcast.34, bf16[2304,128]{1,0:T(8,128)(2,1)} %bitcast.36, f32[1,2048]{1,0:T(1,128)} %bitcast.49, bf16[16,208,2048]{2,1,0:T(8,128)(2,1)} %bitcast.31), custom_call_target="tpu_custom_call" | custom-call | flops 4294967296 | bytes 16777216 | tf_op jit(solution)/shard_map/pallas_call | solution.py:294
  205.3 0.0 copy-start.4
  205.3 4.5 %all-to-all-start.3 = ((bf16[32,144,128]{2,1,0:T(8,128)(2,1)}), bf16[32,144,128]{2,1,0:T(8,128)(2,1)S(1)}, u32[]{:S(2)}, u32[]{:S(2)}) async-start(bf16[32,144,128]{2,1,0:T(8,128)(2,1)} %bitcast.33), calls=%async_computation.3 | async-start | bytes 2359296 | tf_op jit(solution)/shard_map/all_to_all | solution.py:318
  209.8 0.0 copy-done.4
  209.8 0.7 copy.13
  210.5 5.7 %shard_map.122.attended_ref = bf16[128,2048]{1,0:T(8,128)(2,1)} custom-call(bf16[128,2048]{1,0:T(8,128)(2,1)} %bitcast.42, bf16[128,1024]{1,0:T(8,128)(2,1)} %get-tuple-element.10.values_ref, bf16[16,208,2048]{2,1,0:T(8,128)(2,1)} %bitcast.32), custom_call_target="tpu_custom_call" | custom-call | flops 536870912 | bytes 6291456 | tf_op jit(solution)/shard_map/pallas_call | solution.py:322
  216.3 54.8 %all-to-all-done.3 = bf16[32,144,128]{2,1,0:T(8,128)(2,1)S(1)} async-done(((bf16[32,144,128]{2,1,0:T(8,128)(2,1)}), bf16[32,144,128]{2,1,0:T(8,128)(2,1)S(1)}, u32[]{:S(2)}, u32[]{:S(2)}) %all-to-all-start.3) | async-done | bytes 1179680 | tf_op jit(solution)/shard_map/all_to_all | solution.py:318
  271.1 0.0 copy-start
  271.1 1.0 copy-done
  272.2 4.2 %shard_map.124 = bf16[128,2048]{1,0:T(8,128)(2,1)} custom-call(s32[2,128]{1,0:T(2,128)} %get-tuple-element.9.slots_ref, f32[128,2]{1,0:T(8,128)} %bitcast.44, bf16[128,2048]{1,0:T(8,128)(2,1)} %shard_map.122.attended_ref, bf16[4608,128]{1,0:T(8,128)(2,1)} %bitcast.35), custom_call_target="tpu_custom_call" | custom-call | flops 301989888 | bytes 3145728 | tf_op jit(solution)/shard_map/pallas_call | solution.py:334
Async XLA Ops:
  6.5 3.2 %copy-start.3 = (bf16[1,128,576]{1,2,0:T(8,128)(2,1)S(1)}, bf16[1,128,576]{1,2,0:T(8,128)(2,1)}, u32[]{:S(2)}) copy-start(bf16[1,128,576]{1,2,0:T(8,128)(2,1)} %param.14) | copy-start | bytes 442372
  6.5 187.5 %all-gather.3.cloned.1.call-start = ((), (), s32[]{:S(2)}) async-start(), calls=%async_computation.4 | async-start | bytes 14483456 | tf_op jit(solution)/shard_map/all_gather | solution.py:266
  13.2 38.8 %all-to-all-start = ((bf16[16,576,128]{2,1,0:T(8,128)(2,1)}), bf16[16,576,128]{2,1,0:T(8,128)(2,1)S(1)}, u32[]{:S(2)}, u32[]{:S(2)}) async-start(bf16[16,576,128]{2,1,0:T(8,128)(2,1)} %shard_map.119), calls=%async_computation | async-start | bytes 4718592 | tf_op jit(solution)/shard_map/all_to_all | solution.py:242
  52.0 1.4 copy-start.1
  65.5 63.1 %copy-start.2 = (bf16[4608,128]{1,0:T(8,128)(2,1)S(1)}, bf16[4608,128]{1,0:T(8,128)(2,1)}, u32[]{:S(2)}) copy-start(bf16[4608,128]{1,0:T(8,128)(2,1)} %get-tuple-element.11) | copy-start | bytes 3538948
  205.3 4.5 %copy-start.4 = (f32[1,128,2]{1,2,0:T(2,128)S(1)}, f32[1,128,2]{1,2,0:T(2,128)}, u32[]{:S(2)}) copy-start(f32[1,128,2]{1,2,0:T(2,128)} %param.23) | copy-start | bytes 3076
  205.3 65.9 %all-to-all-start.3 = ((bf16[32,144,128]{2,1,0:T(8,128)(2,1)}), bf16[32,144,128]{2,1,0:T(8,128)(2,1)S(1)}, u32[]{:S(2)}, u32[]{:S(2)}) async-start(bf16[32,144,128]{2,1,0:T(8,128)(2,1)} %bitcast.33), calls=%async_computation.3 | async-start | bytes 2359296 | tf_op jit(solution)/shard_map/all_to_all | solution.py:318
  271.1 1.0 copy-start
Sparse Core Ops, SparseCore 0:
  10.4 132.5 all-gather.2

commit v2 on v1

--- a/solution.py
+++ b/solution.py
@@ -56,12 +56,10 @@
 def pack_latent(latent_ref, out_ref):
     tokens = latent_ref.shape[0]
     half = tokens // 2
-    for c in range(out_ref.shape[0]):
-        for j in range(LATENT // LANES):
-            out_ref[c, j * tokens : (j + 1) * tokens, :] = latent_ref[:, j * LANES : (j + 1) * LANES]
-        start = LATENT // LANES * tokens
-        rope = latent_ref[:, LATENT:]
-        out_ref[c, start : start + half, :] = jnp.concatenate([rope[:half], rope[half:]], axis=1)
+    for j in range(LATENT // LANES):
+        out_ref[j * tokens : (j + 1) * tokens, :] = latent_ref[:, j * LANES : (j + 1) * LANES]
+    rope = latent_ref[:, LATENT:]
+    out_ref[LATENT // LANES * tokens :, :] = jnp.concatenate([rope[:half], rope[half:]], axis=1)
 
 
 def dispatch_residual(routes_ref, residual_ref, out_ref, slots_ref, scratch):
@@ -97,32 +95,60 @@
         out_ref[h * tokens : (h + 1) * tokens, LATENT:] = query[:, NOPE:]
 
 
-def attend(place_ref, slots_ref, latent_ref, absorbed_ref, value_up_ref, values_ref, out_ref, keys, scratch):
-    tokens = values_ref.shape[0]
+def lay_keys(blocks, first, keys, tokens):
     half = tokens // 2
-    for c in range(latent_ref.shape[0]):
+    for b in range(blocks.shape[0]):
+        at = (first + b) * tokens
         for j in range(LATENT // LANES):
-            keys[c * tokens : (c + 1) * tokens, j * LANES : (j + 1) * LANES] = latent_ref[
-                c, j * tokens : (j + 1) * tokens, :
-            ]
-        rope = latent_ref[c, LATENT // LANES * tokens : LATENT // LANES * tokens + half, :]
-        keys[c * tokens : c * tokens + half, LATENT:] = rope[:, :ROPE]
-        keys[c * tokens + half : (c + 1) * tokens, LATENT:] = rope[:, ROPE:]
-    span = keys.shape[0]
+            keys[at : at + tokens, j * LANES : (j + 1) * LANES] = blocks[b, j * tokens : (j + 1) * tokens, :]
+        rope = blocks[b, LATENT // LANES * tokens :, :]
+        keys[at : at + half, LATENT:] = rope[:, :ROPE]
+        keys[at + half : at + tokens, LATENT:] = rope[:, ROPE:]
+
+
+def scores(absorbed_ref, keys, key_at, place, g, tokens):
     group = 2 * tokens
-    query_at = lax.broadcasted_iota(jnp.int32, (group, 1), 0) % tokens + place_ref[0] * tokens
-    key_at = lax.broadcasted_iota(jnp.int32, (1, span), 1)
-    allowed = key_at <= query_at
+    query_at = lax.broadcasted_iota(jnp.int32, (group, 1), 0) % tokens + place * tokens
+    score = lax.dot_general(
+        absorbed_ref[g * group : (g + 1) * group, :], keys[...], NT, preferred_element_type=F32
+    )
+    return jnp.where(key_at <= query_at, score * QK ** (-0.5), -1e30)
+
+
+def attend_near(place_ref, key_at_ref, near_ref, up_ref, down_ref, absorbed_ref, sum_ref, highest_ref, denominator_ref, keys):
+    group = absorbed_ref.shape[0] // (HEADS // 2)
+    tokens = group // 2
+    blocks = near_ref.shape[0]
+    for n, ref in enumerate((near_ref, up_ref, down_ref)):
+        lay_keys(ref, n * blocks, keys, tokens)
     for g in range(HEADS // 2):
-        score = lax.dot_general(
-            absorbed_ref[g * group : (g + 1) * group, :], keys[...], NT, preferred_element_type=F32
-        )
-        score = jnp.where(allowed, score * QK ** (-0.5), -1e30)
+        at = slice(g * group, (g + 1) * group)
+        score = scores(absorbed_ref, keys, key_at_ref[...], place_ref[0], g, tokens)
         highest = jnp.max(score, axis=1, keepdims=True)
         expo = jnp.exp(score - highest)
-        denominator = jnp.sum(expo, axis=1, keepdims=True)
+        highest_ref[at, :] = highest
+        denominator_ref[at, :] = jnp.sum(expo, axis=1, keepdims=True)
+        sum_ref[at, :] = jnp.dot(expo.astype(BF16), keys[:, :LATENT], preferred_element_type=F32)
+
+
+def attend_far(
+    place_ref, slots_ref, key_at_ref, first_ref, second_ref, absorbed_ref, sum_ref, highest_ref, denominator_ref,
+    value_up_ref, values_ref, out_ref, keys, scratch,
+):
+    tokens = values_ref.shape[0]
+    group = 2 * tokens
+    lay_keys(first_ref, 0, keys, tokens)
+    lay_keys(second_ref, first_ref.shape[0], keys, tokens)
+    for g in range(HEADS // 2):
+        at = slice(g * group, (g + 1) * group)
+        score = scores(absorbed_ref, keys, key_at_ref[...], place_ref[0], g, tokens)
+        before = highest_ref[at, :]
+        highest = jnp.maximum(before, jnp.max(score, axis=1, keepdims=True))
+        factor = jnp.exp(before - highest)
+        expo = jnp.exp(score - highest)
+        denominator = denominator_ref[at, :] * factor + jnp.sum(expo, axis=1, keepdims=True)
         context = jnp.dot(expo.astype(BF16), keys[:, :LATENT], preferred_element_type=F32)
-        context = (context / denominator).astype(BF16)
+        context = ((context + sum_ref[at, :] * factor) / denominator).astype(BF16)
         for i in range(2):
             h = 2 * g + i
             values_ref[:, h * VHEAD : (h + 1) * VHEAD] = jnp.dot(
@@ -236,11 +262,6 @@
     short_rows = rows * values_width // LANES
     block_rows = tokens * (LATENT + ROPE) // LANES
 
-    latent_out = call(
-        pack_latent, jax.ShapeDtypeStruct((n_ctx, block_rows, LANES), BF16), moved=3 << 20
-    )(latent[0])
-    latent_all = lax.all_to_all(latent_out, "ctx", split_axis=0, concat_axis=0, tiled=True)
-
     residual_out, slots = call(
         dispatch_residual,
         [jax.ShapeDtypeStruct((tall_rows, LANES), BF16), jax.ShapeDtypeStruct((2, tokens), jnp.int32)],
@@ -265,27 +286,64 @@
     )
     packed_all = lax.all_gather(packed, "ctx")
 
+    mine, residual_out = lax.optimization_barrier((latent[0], residual_out))
+    block = call(pack_latent, jax.ShapeDtypeStruct((block_rows, LANES), BF16))(mine)
+    side = 4
+
+    def shift(array, along_x, along_y):
+        pairs = [
+            (x * side + y, (x + along_x) % side * side + (y + along_y) % side)
+            for x in range(side)
+            for y in range(side)
+        ]
+        return lax.ppermute(array, "ctx", pairs)
+
+    near = jnp.stack([block, shift(block, 0, 1), shift(block, 0, -1), shift(block, 0, 2)])
+    up = shift(near, 1, 0)
+    down = shift(near, -1, 0)
+    far_up = shift(up[:2], 1, 0)
+    far_down = shift(down[2:], -1, 0)
+    here = lax.axis_index("ctx").astype(jnp.int32)
+    offsets = [(0, 0), (0, -1), (0, 1), (0, -2)]
+    offsets = [(dx, dy) for dx in (0, -1, 1, -2) for _, dy in offsets]
+    owner = jnp.stack(
+        [(here // side + dx + side) % side * side + (here % side + dy + side) % side for dx, dy in offsets]
+    )
+    key_at = (owner[:, None] * tokens + jnp.arange(tokens, dtype=jnp.int32)[None, :]).reshape(1, n_ctx * tokens)
+    split = 3 * side * tokens
+
     absorbed = call(
         absorb,
         jax.ShapeDtypeStruct((HEADS * tokens, LATENT + ROPE), BF16),
         flops=2 * tokens * HEADS * NOPE * LATENT,
         moved=3 << 20,
     )(queries[0], key_up)
-    place = lax.axis_index("ctx").astype(jnp.int32).reshape(1)
+    place = here.reshape(1)
+    smem = pl.BlockSpec(memory_space=pltpu.SMEM)
+    column = jax.ShapeDtypeStruct((HEADS * tokens, 1), F32)
+    summed, highest, denominator = call(
+        attend_near,
+        [jax.ShapeDtypeStruct((HEADS * tokens, LATENT), F32), column, column],
+        scratch=[pltpu.VMEM((split, LATENT + ROPE), BF16)],
+        flops=3 << 30,
+        moved=6 << 20,
+        in_specs=[smem] + [vmem()] * 5,
+    )(place, key_at[:, :split], near, up, down, absorbed)
     values, values_out = call(
-        attend,
+        attend_far,
         [
             jax.ShapeDtypeStruct((tokens, values_width), BF16),
             jax.ShapeDtypeStruct((short_rows, LANES), BF16),
         ],
         scratch=[
-            pltpu.VMEM((n_ctx * tokens, LATENT + ROPE), BF16),
+            pltpu.VMEM((side * tokens, LATENT + ROPE), BF16),
             pltpu.VMEM((short_rows, LANES), F32),
         ],
-        flops=4 << 30,
+        flops=1 << 30,
         moved=6 << 20,
-        in_specs=[pl.BlockSpec(memory_space=pltpu.SMEM)] + [vmem()] * 4,
-    )(place, slots, latent_all, absorbed, value_up)
+        in_specs=[smem] + [vmem()] * 9,
+    )(place, slots, key_at[:, split:], far_up, far_down, absorbed, summed, highest, denominator, value_up)
+    values_out, residual_rows = lax.optimization_barrier((values_out, residual_rows))
     values_rows = lax.all_to_all(
         values_out.reshape(n_exp, short_rows // n_exp, LANES), "exp", split_axis=0, concat_axis=0, tiled=True
     )

time: 285 us -> 240 us (0.84)
  blocking collectives: 129 us -> 52.2 us
  starting transfers between devices: 12.1 us -> 43.9 us
  waiting for transfers between devices: 80 us -> 72.6 us
  Pallas kernels: 42 us -> 45.4 us
    all_to_all x1 -> x0, blocking collectives: 65.4 us -> none  [body(): lax.all_to_all(residual_out.reshape(n_exp, tall_rows // n_exp, LANES), 'e...]
    all_to_all x1, waiting for transfers between devices: 25.1 us -> 0.01 us  [body(): lax.all_to_all(residual_out.reshape(n_exp, tall_rows // n_exp, LANES), 'e...]
    ppermute x0 -> x7, starting transfers between devices: none -> 23.1 us  [shift(): return lax.ppermute(array, 'ctx', pairs)]
    ppermute x0 -> x7, waiting for transfers between devices: none -> 17.8 us  [shift(): return lax.ppermute(array, 'ctx', pairs)]
    all_to_all x1, blocking collectives: 63.1 us -> 52.2 us  [body(): lax.all_to_all(values_out.reshape(n_exp, short_rows // n_exp, LANES), 'ex...]
    all_to_all x1, starting transfers between devices: 7.58 us -> 16.7 us  [body(): lax.all_to_all(residual_out.reshape(n_exp, tall_rows // n_exp, LANES), 'e...]
    pallas_call x2 -> x3, Pallas kernels: 14.8 us -> 18.2 us  [the longest x1 8.86 us: body(): call(attend_near, [jax.ShapeDtypeStruct((HEADS * tokens, LATENT), F32), c...]
  transfers between devices with their start and end apart: 3 -> 10, of which waited for: 2 -> 6; matrix products, arithmetic and copies ran while one was open for 1% -> 2% of each run, Pallas kernels for 9% -> 13%
where the time goes in v2:
time: 240 us; the launch traced here: 237 us
  waiting for transfers between devices  72.6 us (30%)
  blocking collectives  52.2 us (22%)
  Pallas kernels  45.4 us (19%)
  starting transfers between devices  43.9 us (18%)
  between operations  13.7 us (6%)
  local copies, waits for them, and re-layouts  5.66 us (2%)
  other arithmetic  3.2 us (1%)
    all_to_all x1, waiting for transfers between devices, body(): lax.all_to_all(result.reshape(n_exp, tall_rows // n_exp, LANES), 'exp', s...  54.8 us
    all_to_all x1, blocking collectives, body(): lax.all_to_all(values_out.reshape(n_exp, short_rows // n_exp, LANES), 'ex...  52.2 us
    ppermute x7, starting transfers between devices, shift(): return lax.ppermute(array, 'ctx', pairs)  23.1 us
    ppermute x7, waiting for transfers between devices, shift(): return lax.ppermute(array, 'ctx', pairs)  17.8 us
    all_to_all x1, starting transfers between devices, body(): lax.all_to_all(residual_out.reshape(n_exp, tall_rows // n_exp, LANES), 'e...  16.7 us
    pallas_call x1, Pallas kernels, body(): call(expert, jax.ShapeDtypeStruct((tall_rows, LANES), BF16), scratch=[plt...  11.2 us
    pallas_call x1, Pallas kernels, body(): call(attend_near, [jax.ShapeDtypeStruct((HEADS * tokens, LATENT), F32), c...  8.86 us
    pallas_call x1, Pallas kernels, body(): call(attend_far, [jax.ShapeDtypeStruct((tokens, values_width), BF16), jax...  7.66 us
  transfers between devices with their start and end apart: 10, of which 6 were waited for; matrix products, arithmetic and copies ran while one was open for 2% of the time, Pallas kernels for 13%

profile of v2, /device:TPU:1, one launch (start us, length us, event | category | flops | bytes accessed | tf_op | source)
XLA Modules:
  0.0 236.7 jit_solution(11575776414877654897)
XLA Ops:
  6.5 1.0 copy.18
  7.5 2.1 fusion.6
  9.7 3.3 %shard_map.118 = (bf16[4608,128]{1,0:T(8,128)(2,1)}, s32[2,128]{1,0:T(2,128)}) custom-call(s32[2,128]{1,0:T(2,128)} %bitcast.77, bf16[128,2048]{1,0:T(8,128)(2,1)} %bitcast.63), custom_call_target="tpu_custom_call" | custom-call | flops 150994944 | bytes 3145728 | tf_op jit(solution)/shard_map/pallas_call | solution.py:265
  13.0 16.7 %all-to-all-start = ((bf16[32,144,128]{2,1,0:T(8,128)(2,1)}), bf16[32,144,128]{2,1,0:T(8,128)(2,1)S(1)}, u32[]{:S(2)}, u32[]{:S(2)}) async-start(bf16[32,144,128]{2,1,0:T(8,128)(2,1)} %bitcast.58), calls=%async_computation | async-start | bytes 2359296 | tf_op jit(solution)/shard_map/all_to_all | solution.py:272
  29.7 0.8 copy.14
  30.5 1.6 shard_map.119
  32.2 3.2 %collective-permute-start = (bf16[576,128]{1,0:T(8,128)(2,1)}, bf16[576,128]{1,0:T(8,128)(2,1)S(1)}, u32[]{:S(2)}, u32[]{:S(2)}) collective-permute-start(bf16[576,128]{1,0:T(8,128)(2,1)} %shard_map.119), channel_id=1, source_target_pairs={{0,32},{32,64},{64,96},{96,0},{128,160},{160,192},{192,224},{224,1... | collective-permute-start | bytes 442376 | tf_op jit(solution)/shard_map/ppermute | solution.py:299
  35.4 3.4 %collective-permute-start.1 = (bf16[576,128]{1,0:T(8,128)(2,1)}, bf16[576,128]{1,0:T(8,128)(2,1)S(1)}, u32[]{:S(2)}, u32[]{:S(2)}) collective-permute-start(bf16[576,128]{1,0:T(8,128)(2,1)} %shard_map.119), channel_id=1, source_target_pairs={{0,96},{32,0},{64,32},{96,64},{128,224},{160,128},{192,160},{224,1... | collective-permute-start | bytes 442376 | tf_op jit(solution)/shard_map/ppermute | solution.py:299
  38.7 3.5 %collective-permute-start.2 = (bf16[576,128]{1,0:T(8,128)(2,1)}, bf16[576,128]{1,0:T(8,128)(2,1)S(1)}, u32[]{:S(2)}, u32[]{:S(2)}) collective-permute-start(bf16[576,128]{1,0:T(8,128)(2,1)} %shard_map.119), channel_id=1, source_target_pairs={{0,64},{32,96},{64,0},{96,32},{128,192},{160,224},{192,128},{224,1... | collective-permute-start | bytes 442376 | tf_op jit(solution)/shard_map/ppermute | solution.py:299
  42.3 2.2 collective-permute-done
  44.5 1.8 collective-permute-done.1
  46.3 5.2 %collective-permute-done.2 = bf16[576,128]{1,0:T(8,128)(2,1)S(1)} collective-permute-done((bf16[576,128]{1,0:T(8,128)(2,1)}, bf16[576,128]{1,0:T(8,128)(2,1)S(1)}, u32[]{:S(2)}, u32[]{:S(2)}) %collective-permute-start.2) | collective-permute-done | bytes 147488 | tf_op jit(solution)/shard_map/ppermute | solution.py:299
  51.4 1.0 pad_maximum_fusion.near_ref
  52.4 3.1 %collective-permute-start.3 = (bf16[4,576,128]{2,1,0:T(8,128)(2,1)S(1)}, bf16[4,576,128]{2,1,0:T(8,128)(2,1)S(1)}, u32[]{:S(2)}, u32[]{:S(2)}) collective-permute-start(bf16[4,576,128]{2,1,0:T(8,128)(2,1)S(1)} %pad_maximum_fusion.near_ref), channel_id=1, source_target_pairs={{0,128},{32,160},{64,192},{96,224},{128,256},{160,288},{192,320},{... | collective-permute-start | bytes 1769480 | tf_op jit(solution)/shard_map/ppermute | solution.py:299
  55.6 3.4 %collective-permute-start.5 = (bf16[4,576,128]{2,1,0:T(8,128)(2,1)S(1)}, bf16[4,576,128]{2,1,0:T(8,128)(2,1)S(1)}, u32[]{:S(2)}, u32[]{:S(2)}) collective-permute-start(bf16[4,576,128]{2,1,0:T(8,128)(2,1)S(1)} %pad_maximum_fusion.near_ref), channel_id=1, source_target_pairs={{0,384},{32,416},{64,448},{96,480},{128,0},{160,32},{192,64},{224,... | collective-permute-start | bytes 1769480 | tf_op jit(solution)/shard_map/ppermute | solution.py:299
  59.3 0.6 slice.19.key_at_ref
  60.5 2.9 %shard_map.120.absorbed_ref = bf16[1024,576]{1,0:T(8,128)(2,1)} custom-call(bf16[128,1536]{1,0:T(8,128)(2,1)} %bitcast.65, bf16[512,1024]{1,0:T(8,128)(2,1)} %key_up_ref.1), custom_call_target="tpu_custom_call" | custom-call | flops 134217728 | bytes 3145728 | tf_op jit(solution)/shard_map/pallas_call | solution.py:315
  63.3 5.8 %collective-permute-done.3.up_ref = bf16[4,576,128]{2,1,0:T(8,128)(2,1)S(1)} collective-permute-done((bf16[4,576,128]{2,1,0:T(8,128)(2,1)S(1)}, bf16[4,576,128]{2,1,0:T(8,128)(2,1)S(1)}, u32[]{:S(2)}, u32[]{:S(2)}) %collective-permute-start.3) | collective-permute-done | bytes 589856 | tf_op jit(solution)/shard_map/ppermute | solution.py:299
  69.2 1.9 collective-permute-start.4
  71.2 4.6 %collective-permute-start.6 = (bf16[2,576,128]{2,1,0:T(8,128)(2,1)S(1)}, bf16[2,576,128]{2,1,0:T(8,128)(2,1)S(1)}, u32[]{:S(2)}, u32[]{:S(2)}) collective-permute-start(bf16[2,576,128]{2,1,0:T(8,128)(2,1)S(1)} %slice.18), channel_id=1, source_target_pairs={{0,384},{32,416},{64,448},{96,480},{128,0},{160,32},{192,64},{224,... | collective-permute-start | bytes 884744 | tf_op jit(solution)/shard_map/ppermute | solution.py:299
  75.8 8.9 %shard_map.121 = (f32[1024,512]{1,0:T(8,128)}, f32[1024,1]{1,0:T(8,128)}, f32[1024,1]{1,0:T(8,128)}) custom-call(s32[1]{0:T(128)} %bitcast.4.place_ref, s32[1,1536]{1,0:T(1,128)} %slice.19.key_at_ref, bf16[4,576,128]{2,1,0:T(8,128)(2,1)} %copy-done.2, bf16[4,576,128]{2,1,0:T(8,128)(2,1)} %copy-done.5, bf16[4,576,128]{2,1,0:T(8,128)(2,1)} %copy-done.6, ...), custom_call_target="tpu_custom_call" | custom-call | flops 3221225472 | bytes 6291456 | tf_op jit(solution)/shard_map/pallas_call | solution.py:324
  84.6 2.8 %collective-permute-done.6.second_ref = bf16[2,576,128]{2,1,0:T(8,128)(2,1)S(1)} collective-permute-done((bf16[2,576,128]{2,1,0:T(8,128)(2,1)S(1)}, bf16[2,576,128]{2,1,0:T(8,128)(2,1)S(1)}, u32[]{:S(2)}, u32[]{:S(2)}) %collective-permute-start.6) | collective-permute-done | bytes 294944 | tf_op jit(solution)/shard_map/ppermute | solution.py:299
  87.4 0.7 copy-done.4
  88.2 7.7 %shard_map.122 = (bf16[128,1024]{1,0:T(8,128)(2,1)}, bf16[2304,128]{1,0:T(8,128)(2,1)}) custom-call(s32[1]{0:T(128)} %bitcast.4.place_ref, s32[2,128]{1,0:T(2,128)} %get-tuple-element.15.slots_ref, s32[1,512]{1,0:T(1,128)} %slice.16.key_at_ref, bf16[2,576,128]{2,1,0:T(8,128)(2,1)} %copy-done.3, bf16[2,576,128]{2,1,0:T(8,128)(2,1)} %copy-done.4, ...), custom_call_target="tpu_custom_call" | custom-call | flops 1073741824 | bytes 6291456 | tf_op jit(solution)/shard_map/pallas_call | solution.py:332
  95.8 52.2 %all_to_all.15 = bf16[32,72,128]{2,1,0:T(8,128)(2,1)} all-to-all(bf16[32,72,128]{2,1,0:T(8,128)(2,1)} %bitcast.62), channel_id=1, replica_groups=mesh['ctx'=16,'exp'=32] {'exp'}, dimensions={0} | all-to-all | bytes 1179648 | tf_op jit(solution)/shard_map/all_to_all | solution.py:347
  148.0 11.2 %shard_map.124 = bf16[4608,128]{1,0:T(8,128)(2,1)} custom-call(bf16[4608,128]{1,0:T(8,128)(2,1)} %bitcast.54, bf16[2304,128]{1,0:T(8,128)(2,1)} %bitcast.57, f32[1,2048]{1,0:T(1,128)} %bitcast.76, bf16[16,208,2048]{2,1,0:T(8,128)(2,1)} %bitcast.52), custom_call_target="tpu_custom_call" | custom-call | flops 4294967296 | bytes 16777216 | tf_op jit(solution)/shard_map/pallas_call | solution.py:352
  159.2 4.1 %all-to-all-start.2 = ((bf16[32,144,128]{2,1,0:T(8,128)(2,1)}), bf16[32,144,128]{2,1,0:T(8,128)(2,1)S(1)}, u32[]{:S(2)}, u32[]{:S(2)}) async-start(bf16[32,144,128]{2,1,0:T(8,128)(2,1)} %bitcast.55), calls=%async_computation.2 | async-start | bytes 2359296 | tf_op jit(solution)/shard_map/all_to_all | solution.py:376
  163.3 0.7 copy.13
  164.0 5.8 %shard_map.123.attended_ref = bf16[128,2048]{1,0:T(8,128)(2,1)} custom-call(bf16[128,2048]{1,0:T(8,128)(2,1)} %bitcast.64, bf16[128,1024]{1,0:T(8,128)(2,1)} %get-tuple-element.21.values_ref, bf16[16,208,2048]{2,1,0:T(8,128)(2,1)} %bitcast.53), custom_call_target="tpu_custom_call" | custom-call | flops 536870912 | bytes 6291456 | tf_op jit(solution)/shard_map/pallas_call | solution.py:380
  169.8 54.8 %all-to-all-done.2 = bf16[32,144,128]{2,1,0:T(8,128)(2,1)S(1)} async-done(((bf16[32,144,128]{2,1,0:T(8,128)(2,1)}), bf16[32,144,128]{2,1,0:T(8,128)(2,1)S(1)}, u32[]{:S(2)}, u32[]{:S(2)}) %all-to-all-start.2) | async-done | bytes 1179680 | tf_op jit(solution)/shard_map/all_to_all | solution.py:376
  224.6 1.0 copy-done.1
  225.7 4.2 %shard_map.125 = bf16[128,2048]{1,0:T(8,128)(2,1)} custom-call(s32[2,128]{1,0:T(2,128)} %get-tuple-element.15.slots_ref, f32[128,2]{1,0:T(8,128)} %bitcast.66, bf16[128,2048]{1,0:T(8,128)(2,1)} %shard_map.123.attended_ref, bf16[4608,128]{1,0:T(8,128)(2,1)} %bitcast.56), custom_call_target="tpu_custom_call" | custom-call | flops 301989888 | bytes 3145728 | tf_op jit(solution)/shard_map/pallas_call | solution.py:392
  (28 shorter events, 0.9 us)
Async XLA Ops:
  6.5 141.5 %all-gather.3.cloned.1.call-start = ((), (), s32[]{:S(2)}) async-start(), calls=%async_computation.3 | async-start | bytes 14483456 | tf_op jit(solution)/shard_map/all_gather | solution.py:287
  9.7 20.0 %copy-start.7 = (bf16[1,128,576]{1,2,0:T(8,128)(2,1)S(1)}, bf16[1,128,576]{1,2,0:T(8,128)(2,1)}, u32[]{:S(2)}) copy-start(bf16[1,128,576]{1,2,0:T(8,128)(2,1)} %param.14) | copy-start | bytes 442372
  13.0 82.9 %all-to-all-start = ((bf16[32,144,128]{2,1,0:T(8,128)(2,1)}), bf16[32,144,128]{2,1,0:T(8,128)(2,1)S(1)}, u32[]{:S(2)}, u32[]{:S(2)}) async-start(bf16[32,144,128]{2,1,0:T(8,128)(2,1)} %bitcast.58), calls=%async_computation | async-start | bytes 2359296 | tf_op jit(solution)/shard_map/all_to_all | solution.py:272
  32.2 12.3 %collective-permute-start = (bf16[576,128]{1,0:T(8,128)(2,1)}, bf16[576,128]{1,0:T(8,128)(2,1)S(1)}, u32[]{:S(2)}, u32[]{:S(2)}) collective-permute-start(bf16[576,128]{1,0:T(8,128)(2,1)} %shard_map.119), channel_id=1, source_target_pairs={{0,32},{32,64},{64,96},{96,0},{128,160},{160,192},{192,224},{224,1... | collective-permute-start | bytes 442376 | tf_op jit(solution)/shard_map/ppermute | solution.py:299
  35.4 10.9 %collective-permute-start.1 = (bf16[576,128]{1,0:T(8,128)(2,1)}, bf16[576,128]{1,0:T(8,128)(2,1)S(1)}, u32[]{:S(2)}, u32[]{:S(2)}) collective-permute-start(bf16[576,128]{1,0:T(8,128)(2,1)} %shard_map.119), channel_id=1, source_target_pairs={{0,96},{32,0},{64,32},{96,64},{128,224},{160,128},{192,160},{224,1... | collective-permute-start | bytes 442376 | tf_op jit(solution)/shard_map/ppermute | solution.py:299
  38.7 12.7 %collective-permute-start.2 = (bf16[576,128]{1,0:T(8,128)(2,1)}, bf16[576,128]{1,0:T(8,128)(2,1)S(1)}, u32[]{:S(2)}, u32[]{:S(2)}) collective-permute-start(bf16[576,128]{1,0:T(8,128)(2,1)} %shard_map.119), channel_id=1, source_target_pairs={{0,64},{32,96},{64,0},{96,32},{128,192},{160,224},{192,128},{224,1... | collective-permute-start | bytes 442376 | tf_op jit(solution)/shard_map/ppermute | solution.py:299
  52.4 16.8 %copy-start.2 = (bf16[4,576,128]{2,1,0:T(8,128)(2,1)}, bf16[4,576,128]{2,1,0:T(8,128)(2,1)S(1)}, u32[]{:S(2)}) copy-start(bf16[4,576,128]{2,1,0:T(8,128)(2,1)S(1)} %pad_maximum_fusion.near_ref) | copy-start | bytes 1769476
  52.4 16.7 %collective-permute-start.3 = (bf16[4,576,128]{2,1,0:T(8,128)(2,1)S(1)}, bf16[4,576,128]{2,1,0:T(8,128)(2,1)S(1)}, u32[]{:S(2)}, u32[]{:S(2)}) collective-permute-start(bf16[4,576,128]{2,1,0:T(8,128)(2,1)S(1)} %pad_maximum_fusion.near_ref), channel_id=1, source_target_pairs={{0,128},{32,160},{64,192},{96,224},{128,256},{160,288},{192,320},{... | collective-permute-start | bytes 1769480 | tf_op jit(solution)/shard_map/ppermute | solution.py:299
  55.6 15.6 %collective-permute-start.5 = (bf16[4,576,128]{2,1,0:T(8,128)(2,1)S(1)}, bf16[4,576,128]{2,1,0:T(8,128)(2,1)S(1)}, u32[]{:S(2)}, u32[]{:S(2)}) collective-permute-start(bf16[4,576,128]{2,1,0:T(8,128)(2,1)S(1)} %pad_maximum_fusion.near_ref), channel_id=1, source_target_pairs={{0,384},{32,416},{64,448},{96,480},{128,0},{160,32},{192,64},{224,... | collective-permute-start | bytes 1769480 | tf_op jit(solution)/shard_map/ppermute | solution.py:299
  69.2 6.6 %copy-start.5 = (bf16[4,576,128]{2,1,0:T(8,128)(2,1)}, bf16[4,576,128]{2,1,0:T(8,128)(2,1)S(1)}, u32[]{:S(2)}) copy-start(bf16[4,576,128]{2,1,0:T(8,128)(2,1)S(1)} %collective-permute-done.3.up_ref) | copy-start | bytes 1769476
  69.2 15.4 %collective-permute-start.4 = (bf16[2,576,128]{2,1,0:T(8,128)(2,1)S(1)}, bf16[2,576,128]{2,1,0:T(8,128)(2,1)S(1)}, u32[]{:S(2)}, u32[]{:S(2)}) collective-permute-start(bf16[2,576,128]{2,1,0:T(8,128)(2,1)S(1)} %slice.17), channel_id=1, source_target_pairs={{0,128},{32,160},{64,192},{96,224},{128,256},{160,288},{192,320},{... | collective-permute-start | bytes 884744 | tf_op jit(solution)/shard_map/ppermute | solution.py:299
  71.1 4.6 %copy-start.6 = (bf16[4,576,128]{2,1,0:T(8,128)(2,1)}, bf16[4,576,128]{2,1,0:T(8,128)(2,1)S(1)}, u32[]{:S(2)}) copy-start(bf16[4,576,128]{2,1,0:T(8,128)(2,1)S(1)} %collective-permute-done.5.down_ref) | copy-start | bytes 1769476
  71.2 16.3 %collective-permute-start.6 = (bf16[2,576,128]{2,1,0:T(8,128)(2,1)S(1)}, bf16[2,576,128]{2,1,0:T(8,128)(2,1)S(1)}, u32[]{:S(2)}, u32[]{:S(2)}) collective-permute-start(bf16[2,576,128]{2,1,0:T(8,128)(2,1)S(1)} %slice.18), channel_id=1, source_target_pairs={{0,384},{32,416},{64,448},{96,480},{128,0},{160,32},{192,64},{224,... | collective-permute-start | bytes 884744 | tf_op jit(solution)/shard_map/ppermute | solution.py:299
  84.6 2.8 %copy-start.3 = (bf16[2,576,128]{2,1,0:T(8,128)(2,1)}, bf16[2,576,128]{2,1,0:T(8,128)(2,1)S(1)}, u32[]{:S(2)}) copy-start(bf16[2,576,128]{2,1,0:T(8,128)(2,1)S(1)} %collective-permute-done.4.first_ref) | copy-start | bytes 884740
  87.4 0.7 copy-start.4
  95.8 52.2 %copy-start = (bf16[32,144,128]{2,1,0:T(8,128)(2,1)}, bf16[32,144,128]{2,1,0:T(8,128)(2,1)S(1)}, u32[]{:S(2)}) copy-start(bf16[32,144,128]{2,1,0:T(8,128)(2,1)S(1)} %all-to-all-done) | copy-start | bytes 3538948
  159.2 4.1 %copy-start.8 = (f32[1,128,2]{1,2,0:T(2,128)S(1)}, f32[1,128,2]{1,2,0:T(2,128)}, u32[]{:S(2)}) copy-start(f32[1,128,2]{1,2,0:T(2,128)} %param.23) | copy-start | bytes 3076
  159.2 65.4 %all-to-all-start.2 = ((bf16[32,144,128]{2,1,0:T(8,128)(2,1)}), bf16[32,144,128]{2,1,0:T(8,128)(2,1)S(1)}, u32[]{:S(2)}, u32[]{:S(2)}) async-start(bf16[32,144,128]{2,1,0:T(8,128)(2,1)} %bitcast.55), calls=%async_computation.2 | async-start | bytes 2359296 | tf_op jit(solution)/shard_map/all_to_all | solution.py:376
  224.6 1.0 copy-start.1
Sparse Core Ops, SparseCore 0:
  10.4 126.7 all-gather.2

commit v3 on v1

v3 whole, which is shorter than its diff:
```python
import jax
import jax.numpy as jnp
from jax import lax
from jax.experimental import pallas as pl
from jax.experimental.pallas import tpu as pltpu
from jax.sharding import PartitionSpec as P

D = 2048
HEADS = 8
NOPE = 128
ROPE = 64
QK = NOPE + ROPE
VHEAD = 128
LATENT = 512
FF_DEV = 44
FF_PAD = 48
CAP = 9
LANES = 128
F32 = jnp.float32
BF16 = jnp.bfloat16
NT = (((1,), (1,)), ((), ()))
TN = (((0,), (0,)), ((), ()))


def call(kernel, out_shape, scratch=(), flops=0, moved=0, in_specs=None, limit=16):
    options = {} if in_specs is None else {"in_specs": in_specs}
    return pl.pallas_call(
        kernel,
        out_shape=out_shape,
        scratch_shapes=list(scratch),
        compiler_params=pltpu.CompilerParams(vmem_limit_bytes=limit << 20),
        cost_estimate=pl.CostEstimate(flops=flops, bytes_accessed=moved, transcendentals=0),
        **options,
    )


def vmem():
    return pl.BlockSpec(memory_space=pltpu.VMEM)


def slot_matrix(slots, k, rows):
    return lax.broadcasted_iota(jnp.int32, (rows, slots.shape[1]), 0) == slots[k : k + 1, :]


def both_choices(slots, rows):
    return (slot_matrix(slots, 0, rows) | slot_matrix(slots, 1, rows)).astype(BF16)


def put_column(j, column, blocks):
    count = blocks.shape[0]
    parts = blocks.shape[1] // CAP
    blocks[:, 8 * j : 8 * j + 8, :] = column[: 8 * count].reshape(count, 8, LANES)
    blocks[:, 8 * parts + j, :] = column[8 * count :]


def put_pair(j, chunk, extra, out_ref):
    count = extra.shape[0]
    columns = [chunk[:, :LANES], chunk[:, LANES:]]
    whole = jnp.concatenate([c[: 8 * count].reshape(count, 8, LANES) for c in columns], axis=1)
    out_ref[:, 8 * j : 8 * j + 16, :] = whole.astype(BF16)
    for n, c in enumerate(columns):
        extra[:, j + n, :] = c[8 * count :]


def take_column(j, blocks):
    count = blocks.shape[0]
    parts = blocks.shape[1] // CAP
    whole = blocks[:, 8 * j : 8 * j + 8, :].reshape(8 * count, LANES)
    return jnp.concatenate([whole, blocks[:, 8 * parts + j, :]], axis=0)


def load_blocks(source_ref, blocks):
    blocks[...] = source_ref[...].astype(F32).reshape(blocks.shape)


def store_blocks(blocks, out_ref):
    out_ref[...] = blocks[...].reshape(out_ref.shape).astype(BF16)


def fill_rows(matrix, source_ref, blocks, out_ref):
    for j in range(0, source_ref.shape[1] // LANES, 2):
        chunk = jnp.dot(matrix, source_ref[:, j * LANES : (j + 2) * LANES], preferred_element_type=F32)
        put_column(j, chunk[:, :LANES], blocks)
        put_column(j + 1, chunk[:, LANES:], blocks)
    store_blocks(blocks, out_ref)


def begin(
    core_ref, projection_ref, gate_ref, up_ref, down_ref, routes_ref, residual_ref,
    packed_ref, out_ref, slots_ref, extra,
):
    columns = projection_ref[...].T
    part = columns.shape[0] // 4
    depth = columns.shape[1]
    columns = jnp.where(core_ref[0] == 0, columns[: 2 * part], columns[2 * part :])
    packed_ref[:part, :depth] = columns[:part]
    packed_ref[:part, depth:] = columns[part:]
    zeros = jnp.zeros((FF_PAD - FF_DEV, D), BF16)
    for n, ref in enumerate((gate_ref, up_ref, down_ref)):
        packed_ref[part + n * FF_PAD : part + (n + 1) * FF_PAD, :] = jnp.concatenate([ref[...], zeros], axis=0)
    tokens = routes_ref.shape[1]
    count = extra.shape[0]
    rows = count * CAP
    expert = lax.broadcasted_iota(jnp.int32, (LANES, tokens), 0)
    first = (expert == routes_ref[0:1, :]).astype(F32)
    second = (expert == routes_ref[1:2, :]).astype(F32)
    row = lax.broadcasted_iota(jnp.int32, (tokens, tokens), 0)
    column = lax.broadcasted_iota(jnp.int32, (tokens, tokens), 1)
    before = (row < column).astype(BF16)
    count_first = jnp.dot(first.astype(BF16), before, preferred_element_type=F32)
    count_second = jnp.dot(second.astype(BF16), before, preferred_element_type=F32)
    count_second = count_second + jnp.sum(first, axis=1, keepdims=True)
    place_first = jnp.sum(count_first * first, axis=0, keepdims=True).astype(jnp.int32)
    place_second = jnp.sum(count_second * second, axis=0, keepdims=True).astype(jnp.int32)
    chosen = routes_ref[...]
    place = jnp.concatenate([place_first, place_second], axis=0)
    slots = jnp.where(place < 8, chosen * 8 + place, 8 * count + chosen)
    slots_ref[...] = slots
    matrix = both_choices(slots, rows)
    for j in range(0, D // LANES, 2):
        chunk = jnp.dot(matrix, residual_ref[:, j * LANES : (j + 2) * LANES], preferred_element_type=F32)
        put_pair(j, chunk, extra, out_ref)
    out_ref[:, 8 * D // LANES :, :] = extra[...].astype(BF16)


def absorb(queries_ref, key_up_ref, out_ref):
    tokens = queries_ref.shape[0]
    for h in range(HEADS):
        query = queries_ref[:, h * QK : (h + 1) * QK]
        keys = key_up_ref[:, h * NOPE : (h + 1) * NOPE]
        out_ref[h * tokens : (h + 1) * tokens, :LATENT] = lax.dot_general(
            query[:, :NOPE], keys, NT, preferred_element_type=F32
        ).astype(BF16)
        out_ref[h * tokens : (h + 1) * tokens, LATENT:] = query[:, NOPE:]


def attend(key_at_ref, place_ref, absorbed_ref, keys, state, g):
    group = absorbed_ref.shape[0] // (HEADS // 2)
    tokens = group // 2
    query_at = lax.broadcasted_iota(jnp.int32, (group, 1), 0) % tokens + place_ref[0] * tokens
    score = jnp.dot(absorbed_ref[g * group : (g + 1) * group, :], keys[...], preferred_element_type=F32)
    score = jnp.where(key_at_ref[...] <= query_at, score * QK ** (-0.5), -1e30)
    highest = jnp.max(score, axis=1, keepdims=True)
    if state is not None:
        highest = jnp.maximum(highest, state[1])
    expo = jnp.exp(score - highest)
    denominator = jnp.sum(expo, axis=1, keepdims=True)
    summed = lax.dot_general(expo.astype(BF16), keys[:LATENT, :], NT, preferred_element_type=F32)
    if state is not None:
        factor = jnp.exp(state[1] - highest)
        summed = summed + state[0] * factor
        denominator = denominator + state[2] * factor
    return summed, highest, denominator


def lay_keys(refs, keys):
    at = 0
    for ref in refs:
        for b in range(ref.shape[0]):
            keys[:, at : at + ref.shape[2]] = ref[b]
            at += ref.shape[2]


def attend_first(place_ref, key_at_ref, near_ref, absorbed_ref, sum_ref, stats_ref, keys):
    lay_keys((near_ref,), keys)
    group = absorbed_ref.shape[0] // (HEADS // 2)
    for g in range(HEADS // 2):
        at = slice(g * group, (g + 1) * group)
        summed, highest, denominator = attend(key_at_ref, place_ref, absorbed_ref, keys, None, g)
        sum_ref[at, :] = summed
        stats_ref[at, 0:1] = highest
        stats_ref[at, 1:2] = denominator


def attend_more(
    place_ref, key_at_ref, up_ref, down_ref, absorbed_ref, sum_in_ref, stats_in_ref, sum_ref, stats_ref, keys
):
    lay_keys((up_ref, down_ref), keys)
    group = absorbed_ref.shape[0] // (HEADS // 2)
    for g in range(HEADS // 2):
        at = slice(g * group, (g + 1) * group)
        state = (sum_in_ref[at, :], stats_in_ref[at, 0:1], stats_in_ref[at, 1:2])
        summed, highest, denominator = attend(key_at_ref, place_ref, absorbed_ref, keys, state, g)
        sum_ref[at, :] = summed
        stats_ref[at, 0:1] = highest
        stats_ref[at, 1:2] = denominator


def attend_last(
    place_ref, slots_ref, key_at_ref, up_ref, down_ref, absorbed_ref, sum_in_ref, stats_in_ref,
    value_up_ref, values_ref, out_ref, keys, scratch,
):
    lay_keys((up_ref, down_ref), keys)
    tokens = values_ref.shape[0]
    group = 2 * tokens
    for g in range(HEADS // 2):
        at = slice(g * group, (g + 1) * group)
        state = (sum_in_ref[at, :], stats_in_ref[at, 0:1], stats_in_ref[at, 1:2])
        summed, highest, denominator = attend(key_at_ref, place_ref, absorbed_ref, keys, state, g)
        context = (summed / denominator).astype(BF16)
        for i in range(2):
            h = 2 * g + i
            values_ref[:, h * VHEAD : (h + 1) * VHEAD] = jnp.dot(
                context[i * tokens : (i + 1) * tokens],
                value_up_ref[:, h * VHEAD : (h + 1) * VHEAD],
                preferred_element_type=F32,
            ).astype(BF16)
    fill_rows(both_choices(slots_ref[...], scratch.shape[0] * CAP), values_ref, scratch, out_ref)


def unpack(blocks, parts, store):
    for j in range(parts):
        store[:, j * LANES : (j + 1) * LANES] = take_column(j, blocks).astype(BF16)


def start_all(pairs, sems):
    copies = [pltpu.make_async_copy(source, target, sems.at[n]) for n, (source, target) in enumerate(pairs)]
    for copy in copies:
        copy.start()
    return copies


def projection_pairs(core_ref, own_ref, other_ref, projection):
    part = projection.shape[1] // 4
    depth = projection.shape[2]
    pairs = []
    for n in range(4):
        ref, half = (own_ref, core_ref[0]) if n < 2 else (other_ref, 1 - core_ref[0])
        row = pl.multiple_of(half * (2 * part) + n % 2 * part, part)
        source = ref.at[:, 0:part, n % 2 * depth : (n % 2 + 1) * depth]
        pairs.append((source, projection.at[:, pl.ds(row, part), :]))
    return pairs


def take_part(packed_ref, part_ref, sem):
    copy = pltpu.make_async_copy(packed_ref.at[:, 0 : part_ref.shape[1], :], part_ref, sem)
    copy.start()
    copy.wait()


def project(values, projection):
    flat = projection[...].reshape(D, projection.shape[2])
    return lax.dot_general(values, flat, NT, preferred_element_type=F32)


def expert(
    core_ref, gain_ref, residual_ref, values_ref, packed_ref, other_ref, out_ref,
    residual_rows, value_rows, projection, gate, up, down, tall, short, residual, values, extra, sems,
):
    start = projection.shape[1] // 4
    pairs = [(values_ref, value_rows), (residual_ref, residual_rows)]
    pairs += projection_pairs(core_ref, packed_ref, other_ref, projection)
    pairs += [
        (packed_ref.at[:, start + n * FF_PAD : start + (n + 1) * FF_PAD, :], buffer)
        for n, buffer in enumerate((gate, up, down))
    ]
    copies = [pltpu.make_async_copy(source, target, sems.at[n]) for n, (source, target) in enumerate(pairs)]
    for copy in copies[:6]:
        copy.start()
    copies[0].wait()
    copies[6].start()
    load_blocks(value_rows, short)
    unpack(short, values.shape[1] // LANES, values)
    copies[1].wait()
    load_blocks(residual_rows, tall)
    unpack(tall, D // LANES, residual)
    for copy in copies[2:6]:
        copy.wait()
    copies[7].start()
    product = project(values[...], projection)
    attended = (residual[...].astype(F32) + product).astype(BF16).astype(F32)
    scale = lax.rsqrt(jnp.mean(attended * attended, axis=1, keepdims=True) + 1e-06)
    normed = (attended * scale * gain_ref[...]).astype(BF16)
    units = gate.shape[0] * gate.shape[1]
    copies[6].wait()
    copies[8].start()
    gate_proj = lax.dot_general(normed, gate[...].reshape(units, D), NT, preferred_element_type=F32)
    copies[7].wait()
    up_proj = lax.dot_general(normed, up[...].reshape(units, D), NT, preferred_element_type=F32)
    activation = (gate_proj / (1.0 + jnp.exp(-gate_proj)) * up_proj).astype(BF16)
    copies[8].wait()
    for j in range(0, D // LANES, 2):
        columns = down[:, :, j * LANES : (j + 2) * LANES].reshape(units, 2 * LANES)
        put_pair(j, jnp.dot(activation, columns, preferred_element_type=F32), extra, out_ref)
    out_ref[:, 8 * D // LANES :, :] = extra[...].astype(BF16)


def home(core_ref, residual_ref, values_ref, packed_ref, other_ref, out_ref, projection, sems):
    for copy in start_all(projection_pairs(core_ref, packed_ref, other_ref, projection), sems):
        copy.wait()
    projected = project(values_ref[...], projection)
    out_ref[...] = (residual_ref[...].astype(F32) + projected).astype(BF16)


def combine(slots_ref, weights_ref, attended_ref, rows_ref, out_ref, blocks, attended, result, sems):
    copy = pltpu.make_async_copy(attended_ref, attended, sems.at[0])
    copy.start()
    slots = slots_ref[...]
    tokens = slots.shape[1]
    rows = blocks.shape[0] * CAP
    first = slot_matrix(slots, 0, rows).astype(BF16)
    second = slot_matrix(slots, 1, rows).astype(BF16)
    same = lax.broadcasted_iota(jnp.int32, (tokens, tokens), 0) == lax.broadcasted_iota(
        jnp.int32, (tokens, tokens), 1
    )
    weights = [jnp.sum(jnp.where(same, weights_ref[k : k + 1, :], 0.0), axis=1, keepdims=True) for k in range(2)]
    load_blocks(rows_ref, blocks)
    copy.wait()
    copies = []
    for j in range(0, D // LANES, 2):
        pair = jnp.concatenate([take_column(j, blocks), take_column(j + 1, blocks)], axis=1).astype(BF16)
        picked_first = lax.dot_general(first, pair, TN, preferred_element_type=F32)
        picked_second = lax.dot_general(second, pair, TN, preferred_element_type=F32)
        mixed = picked_first * weights[0] + picked_second * weights[1]
        at = slice(j * LANES, (j + 2) * LANES)
        result[:, at] = (attended[:, at].astype(F32) + mixed).astype(BF16)
        if j % 4 == 2:
            at = slice((j - 2) * LANES, (j + 2) * LANES)
            copies.append(pltpu.make_async_copy(result.at[:, at], out_ref.at[:, at], sems.at[1 + j // 4]))
            copies[-1].start()
    for copy in copies:
        copy.wait()


def body(
    residual, queries, latent, key_up, value_up, out_proj, norm_gain,
    w_gate, w_up, w_down, routes, route_weights,
):
    tokens = residual.shape[1]
    n_ctx = lax.axis_size("ctx")
    n_exp = lax.axis_size("exp")
    rows = n_exp * CAP
    values_width = HEADS * VHEAD
    tall_rows = rows * D // LANES
    short_rows = rows * values_width // LANES
    tall = pltpu.VMEM((n_exp, tall_rows // n_exp, LANES), F32)
    extra = pltpu.VMEM((n_exp, D // LANES, LANES), F32)
    short = pltpu.VMEM((n_exp, short_rows // n_exp, LANES), F32)

    smem = pl.BlockSpec(memory_space=pltpu.SMEM)
    core = (lax.axis_index("exp").astype(jnp.int32) % 2).reshape(1)
    part = out_proj.shape[1] // 4
    packed, residual_out, slots = call(
        begin,
        [
            jax.ShapeDtypeStruct((part + 3 * FF_PAD, D), BF16),
            jax.ShapeDtypeStruct((n_exp, tall_rows // n_exp, LANES), BF16),
            jax.ShapeDtypeStruct((2, tokens), jnp.int32),
        ],
        scratch=[extra],
        flops=2 * rows * tokens * D,
        moved=3 << 20,
        in_specs=[smem] + [vmem()] * 6,
        limit=60,
    )(core, out_proj, w_gate[0].T, w_up[0].T, w_down[0], routes[0].T, residual[0])
    packed_all = lax.all_gather(packed, "ctx")
    residual_rows = lax.all_to_all(residual_out, "exp", split_axis=0, concat_axis=0, tiled=True)

    block, residual_out = lax.optimization_barrier((latent[0].T, residual_out))
    side = 4

    def send(array, columns):
        pairs = [(x * side + y, to * side + y) for x, to in columns for y in range(side)]
        return lax.ppermute(array, "ctx", pairs)

    rows_of_y = [[x * side + y for y in range(side)] for x in range(side)]
    near = lax.all_gather(block, "ctx", axis_index_groups=rows_of_y)
    up = send(near, [(0, 1), (1, 2), (2, 3)])
    down = send(near, [(0, 3), (1, 0)])
    far_up = send(up[:2], [(1, 2), (2, 3)])
    far_down = send(down[2:], [(0, 3), (3, 2)])
    here = lax.axis_index("ctx").astype(jnp.int32)
    owner = [(here // side + dx + side) % side * side + y for dx in (0, -1, 1, -2) for y in range(side)]
    key_at = (jnp.stack(owner)[:, None] * tokens + jnp.arange(tokens, dtype=jnp.int32)[None, :]).reshape(1, -1)
    third = side * tokens

    absorbed = call(
        absorb,
        jax.ShapeDtypeStruct((HEADS * tokens, LATENT + ROPE), BF16),
        flops=2 * tokens * HEADS * NOPE * LATENT,
        moved=3 << 20,
    )(queries[0], key_up)
    place = here.reshape(1)
    width = LATENT + ROPE
    state = [
        jax.ShapeDtypeStruct((HEADS * tokens, LATENT), F32),
        jax.ShapeDtypeStruct((HEADS * tokens, 2), F32),
    ]
    summed, stats = call(
        attend_first,
        state,
        scratch=[pltpu.VMEM((width, third), BF16)],
        flops=1 << 30,
        moved=6 << 20,
        in_specs=[smem] + [vmem()] * 3,
    )(place, key_at[:, :third], near, absorbed)
    summed, stats = call(
        attend_more,
        state,
        scratch=[pltpu.VMEM((width, 2 * third), BF16)],
        flops=2 << 30,
        moved=6 << 20,
        in_specs=[smem] + [vmem()] * 6,
        limit=24,
    )(place, key_at[:, third : 3 * third], up, down, absorbed, summed, stats)
    values, values_out = call(
        attend_last,
        [
            jax.ShapeDtypeStruct((tokens, values_width), BF16),
            jax.ShapeDtypeStruct((short_rows, LANES), BF16),
        ],
        scratch=[pltpu.VMEM((width, third), BF16), short],
        flops=1 << 30,
        moved=6 << 20,
        in_specs=[smem] + [vmem()] * 8,
        limit=20,
    )(place, slots, key_at[:, 3 * third :], far_up, far_down, absorbed, summed, stats, value_up)
    values_out, residual_rows = lax.optimization_barrier((values_out, residual_rows))
    values_rows = lax.all_to_all(
        values_out.reshape(n_exp, short_rows // n_exp, LANES), "exp", split_axis=0, concat_axis=0, tiled=True
    )

    any_space = pl.BlockSpec(memory_space=pl.ANY)
    projection = pltpu.VMEM((n_ctx, 4 * part, values_width), BF16)
    own_part = call(
        take_part,
        jax.ShapeDtypeStruct((n_ctx, part, D), BF16),
        scratch=[pltpu.SemaphoreType.DMA],
        moved=4 << 20,
        in_specs=[any_space],
        limit=60,
    )(packed_all)
    other_part = lax.ppermute(own_part, "exp", [(e, e + 1 - 2 * (e % 2)) for e in range(n_exp)])
    result = call(
        expert,
        jax.ShapeDtypeStruct((n_exp, tall_rows // n_exp, LANES), BF16),
        scratch=[pltpu.VMEM((tall_rows, LANES), BF16), pltpu.VMEM((short_rows, LANES), BF16), projection]
        + [pltpu.VMEM((n_ctx, FF_PAD, D), BF16)] * 3
        + [tall, short, pltpu.VMEM((rows, D), BF16), pltpu.VMEM((rows, values_width), BF16)]
        + [extra, pltpu.SemaphoreType.DMA((9,))],
        flops=4 << 30,
        moved=16 << 20,
        in_specs=[smem, vmem()] + [any_space] * 4,
        limit=60,
    )(
        core,
        norm_gain.reshape(1, D),
        residual_rows.reshape(tall_rows, LANES),
        values_rows.reshape(short_rows, LANES),
        packed_all,
        other_part,
    )
    returned = lax.all_to_all(
        result, "exp", split_axis=0, concat_axis=0, tiled=True
    )

    attended = call(
        home,
        jax.ShapeDtypeStruct((tokens, D), BF16),
        scratch=[projection, pltpu.SemaphoreType.DMA((4,))],
        flops=2 * tokens * D * values_width,
        moved=6 << 20,
        in_specs=[smem, vmem(), vmem(), any_space, any_space],
        limit=60,
    )(core, residual[0], values, packed_all, other_part)
    layer_out = pl.pallas_call(
        combine,
        out_shape=jax.ShapeDtypeStruct((tokens, D), BF16),
        in_specs=[vmem(), vmem(), any_space, vmem()],
        out_specs=any_space,
        scratch_shapes=[tall, pltpu.VMEM((tokens, D), BF16), pltpu.VMEM((tokens, D), BF16)]
        + [pltpu.SemaphoreType.DMA((5,))],
        input_output_aliases={2: 0},
        compiler_params=pltpu.CompilerParams(vmem_limit_bytes=16 << 20),
        cost_estimate=pl.CostEstimate(flops=4 * rows * tokens * D, bytes_accessed=3 << 20, transcendentals=0),
    )(slots, route_weights[0].T, attended, returned.reshape(tall_rows, LANES))
    return layer_out[None]


def solution(mesh):
    return jax.shard_map(
        body,
        mesh=mesh,
        in_specs=(
            P("exp", "ctx", None),
            P("exp", "ctx", None),
            P("exp", "ctx", None),
            P(),
            P(),
            P(None, "ctx"),
            P(),
            P("exp", None, "ctx"),
            P("exp", None, "ctx"),
            P("exp", "ctx", None),
            P("exp", "ctx", None),
            P("exp", "ctx", None),
        ),
        out_specs=P("exp", "ctx", None),
        check_vma=False,
    )
```

time: 285 us -> 226 us (0.79)
  blocking collectives: 129 us -> 12.1 us
  starting transfers between devices: 12.1 us -> 49.7 us
  waiting for transfers between devices: 80 us -> 110 us
  Pallas kernels: 42 us -> 37.8 us
    all_to_all x2 -> x0, blocking collectives: 129 us -> none  [the longest x1 65.4 us: body(): lax.all_to_all(residual_out.reshape(n_exp, tall_rows // n_exp, LANES), 'e...]
    all_gather x1, waiting for transfers between devices: 0.01 us -> 26.1 us  [body(): packed_all = lax.all_gather(packed, 'ctx')]
    all_to_all x2 -> x3, starting transfers between devices: 12.1 us -> 35.2 us  [the longest x1 16.9 us: body(): lax.all_to_all(residual_out, 'exp', split_axis=0, concat_axis=0, tiled=True)]
    ppermute x0 -> x5, waiting for transfers between devices: none -> 15 us  [the longest x4 15 us: send(): return lax.ppermute(array, 'ctx', pairs)]
    ppermute x0 -> x5, starting transfers between devices: none -> 14.5 us  [the longest x4 11.7 us: send(): return lax.ppermute(array, 'ctx', pairs)]
    all_gather x0 -> x1, blocking collectives: none -> 12.1 us  [body(): near = lax.all_gather(block, 'ctx', axis_index_groups=rows_of_y)]
    all_to_all x2 -> x3, waiting for transfers between devices: 79.9 us -> 68.5 us  [the longest x1 55.6 us: body(): lax.all_to_all(result, 'exp', split_axis=0, concat_axis=0, tiled=True)]
    pallas_call x6 -> x8, Pallas kernels: 39.1 us -> 37.4 us  [the longest x1 10.3 us: body(): call(expert, jax.ShapeDtypeStruct((n_exp, tall_rows // n_exp, LANES), BF1...]
  transfers between devices with their start and end apart: 3 -> 9, of which waited for: 2 -> 6; matrix products, arithmetic and copies ran while one was open for 1% -> 0% of each run, Pallas kernels for 9% -> 10%
where the time goes in v3:
time: 226 us
  waiting for transfers between devices  110 us (49%)
  starting transfers between devices  49.7 us (22%)
  Pallas kernels  37.8 us (17%)
  between operations  13.7 us (6%)
  blocking collectives  12.1 us (5%)
  local copies, waits for them, and re-layouts  2.5 us (1%)
    all_to_all x1, waiting for transfers between devices, body(): lax.all_to_all(result, 'exp', split_axis=0, concat_axis=0, tiled=True)  55.6 us
    all_gather x1, waiting for transfers between devices, body(): packed_all = lax.all_gather(packed, 'ctx')  26.1 us
    all_to_all x1, starting transfers between devices, body(): lax.all_to_all(residual_out, 'exp', split_axis=0, concat_axis=0, tiled=True)  16.9 us
    ppermute x4, waiting for transfers between devices, send(): return lax.ppermute(array, 'ctx', pairs)  15 us
    all_gather x1, blocking collectives, body(): near = lax.all_gather(block, 'ctx', axis_index_groups=rows_of_y)  12.1 us
    all_to_all x1, starting transfers between devices, body(): lax.all_to_all(result, 'exp', split_axis=0, concat_axis=0, tiled=True)  12 us
    ppermute x4, starting transfers between devices, send(): return lax.ppermute(array, 'ctx', pairs)  11.7 us
    pallas_call x1, Pallas kernels, body(): call(expert, jax.ShapeDtypeStruct((n_exp, tall_rows // n_exp, LANES), BF1...  10.3 us
  transfers between devices with their start and end apart: 9, of which 6 were waited for; matrix products, arithmetic and copies ran while one was open for 0% of the time, Pallas kernels for 10%

profile of v3, /device:TPU:1, one launch (start us, length us, event | category | flops | bytes accessed | tf_op | source)
XLA Modules:
  0.0 225.5 jit_solution(17814128540759655222)
XLA Ops:
  6.5 3.5 %shard_map.118 = (bf16[176,2048]{1,0:T(8,128)(2,1)}, bf16[32,144,128]{2,1,0:T(8,128)(2,1)}, s32[2,128]{1,0:T(2,128)}) custom-call(s32[1]{0:T(128)} %bitcast.core_ref, bf16[1024,128]{1,0:T(8,128)(2,1)} %projection_ref.1, bf16[44,2048]{1,0:T(8,128)(2,1)} %bitcast.57, bf16[44,2048]{1,0:T(8,128)(2,1)} %bitcast.58, bf16[44,2048]{1,0:T(8,128)(2,1)} %bitcast.59, ...), custom_call_target="tpu_custom_call" | custom-call | flops 150994944 | bytes 3145728 | tf_op jit(solution)/shard_map/pallas_call | solution.py:343
  10.0 0.0 all-gather.4.cloned.1.call-update
  10.1 16.9 %all-to-all-start = ((bf16[32,144,128]{2,1,0:T(8,128)(2,1)}), bf16[32,144,128]{2,1,0:T(8,128)(2,1)}, u32[]{:S(2)}, u32[]{:S(2)}) async-start(bf16[32,144,128]{2,1,0:T(8,128)(2,1)} %get-tuple-element.18), calls=%async_computation | async-start | bytes 2359296 | tf_op jit(solution)/shard_map/all_to_all | solution.py:357
  27.0 12.1 %all-gather = bf16[2304,128]{1,0:T(8,128)(2,1)S(1)} all-gather(bf16[576,128]{1,0:T(8,128)(2,1)S(1)} %bitcast.60), channel_id=2, replica_groups={{0,32,64,96},{128,160,192,224},{256,288,320,352},{384,416,448,480},{1,3..., dimensions={0}, use_global_device_ids=true | all-gather | bytes 737280 | tf_op jit(solution)/shard_map/all_gather | solution.py:367
  39.1 3.1 %collective-permute-start = (bf16[4,576,128]{2,1,0:T(8,128)(2,1)S(1)}, bf16[4,576,128]{2,1,0:T(8,128)(2,1)S(1)}, u32[]{:S(2)}, u32[]{:S(2)}) collective-permute-start(bf16[4,576,128]{2,1,0:T(8,128)(2,1)S(1)} %bitcast.46), channel_id=1, source_target_pairs={{0,128},{32,160},{64,192},{96,224},{128,256},{160,288},{192,320},{... | collective-permute-start | bytes 1769480 | tf_op jit(solution)/shard_map/ppermute | solution.py:364
  42.3 2.9 %collective-permute-start.2 = (bf16[4,576,128]{2,1,0:T(8,128)(2,1)S(1)}, bf16[4,576,128]{2,1,0:T(8,128)(2,1)S(1)}, u32[]{:S(2)}, u32[]{:S(2)}) collective-permute-start(bf16[4,576,128]{2,1,0:T(8,128)(2,1)S(1)} %bitcast.47), channel_id=1, source_target_pairs={{0,384},{32,416},{64,448},{96,480},{128,0},{160,32},{192,64},{224,... | collective-permute-start | bytes 1769480 | tf_op jit(solution)/shard_map/ppermute | solution.py:364
  45.2 0.1 stack.67
  45.3 0.1 iota_add_fusion
  45.4 0.5 shard_map.119.absorbed_ref
  45.9 13.5 %collective-permute-done.up_ref = bf16[4,576,128]{2,1,0:T(8,128)(2,1)S(1)} collective-permute-done((bf16[4,576,128]{2,1,0:T(8,128)(2,1)S(1)}, bf16[4,576,128]{2,1,0:T(8,128)(2,1)S(1)}, u32[]{:S(2)}, u32[]{:S(2)}) %collective-permute-start) | collective-permute-done | bytes 589856 | tf_op jit(solution)/shard_map/ppermute | solution.py:364
  59.4 0.7 collective-permute-start.1
  60.1 1.5 collective-permute-done.2.down_ref
  61.6 5.1 %collective-permute-start.3 = (bf16[2,576,128]{2,1,0:T(8,128)(2,1)S(1)}, bf16[2,576,128]{2,1,0:T(8,128)(2,1)S(1)}, u32[]{:S(2)}, u32[]{:S(2)}) collective-permute-start(bf16[2,576,128]{2,1,0:T(8,128)(2,1)S(1)} %slice.22), channel_id=1, source_target_pairs={{0,384},{32,416},{64,448},{96,480},{384,256},{416,288},{448,320},{... | collective-permute-start | bytes 884744 | tf_op jit(solution)/shard_map/ppermute | solution.py:364
  66.7 2.3 %shard_map.120 = (f32[1024,512]{1,0:T(8,128)S(1)}, f32[1024,2]{1,0:T(8,128)S(1)}) custom-call(s32[1]{0:T(128)} %bitcast.11.place_ref, s32[1,512]{1,0:T(1,128)S(1)} %get-tuple-element.29.key_at_ref, bf16[4,576,128]{2,1,0:T(8,128)(2,1)S(1)} %bitcast.48, bf16[1024,576]{1,0:T(8,128)(2,1)S(1)} %shard_map.119.absorbed_ref), custom_call_target="tpu_custom_call" | custom-call | flops 1073741824 | bytes 6291456 | tf_op jit(solution)/shard_map/pallas_call | solution.py:389
  69.0 0.0 copy-start.4
  69.0 4.6 %shard_map.121 = (f32[1024,512]{1,0:T(8,128)S(1)}, f32[1024,2]{1,0:T(8,128)S(1)}) custom-call(s32[1]{0:T(128)} %bitcast.11.place_ref, s32[1,1024]{1,0:T(1,128)S(1)} %slice.23.key_at_ref, bf16[4,576,128]{2,1,0:T(8,128)(2,1)S(1)} %collective-permute-done.up_ref, bf16[4,576,128]{2,1,0:T(8,128)(2,1)S(1)} %collective-permute-done.2.down_ref, ...), custom_call_target="tpu_custom_call" | custom-call | flops 2147483648 | bytes 6291456 | tf_op jit(solution)/shard_map/pallas_call | solution.py:397
  73.6 5.5 %shard_map.122 = (bf16[128,1024]{1,0:T(8,128)(2,1)S(1)}, bf16[2304,128]{1,0:T(8,128)(2,1)}) custom-call(s32[1]{0:T(128)} %bitcast.11.place_ref, s32[2,128]{1,0:T(2,128)S(1)} %copy-done.4, s32[1,512]{1,0:T(1,128)S(1)} %get-tuple-element.30.key_at_ref, bf16[2,576,128]{2,1,0:T(8,128)(2,1)S(1)} %collective-permute-done.1.up_ref, ...), custom_call_target="tpu_custom_call" | custom-call | flops 1073741824 | bytes 6291456 | tf_op jit(solution)/shard_map/pallas_call | solution.py:406
  79.1 0.7 copy-done.3
  79.8 8.5 %all-to-all-done = bf16[32,144,128]{2,1,0:T(8,128)(2,1)} async-done(((bf16[32,144,128]{2,1,0:T(8,128)(2,1)}), bf16[32,144,128]{2,1,0:T(8,128)(2,1)}, u32[]{:S(2)}, u32[]{:S(2)}) %all-to-all-start) | async-done | bytes 1179680 | tf_op jit(solution)/shard_map/all_to_all | solution.py:357
  88.4 6.3 %all-to-all-start.1 = ((bf16[32,72,128]{2,1,0:T(8,128)(2,1)}), bf16[32,72,128]{2,1,0:T(8,128)(2,1)S(1)}, u32[]{:S(2)}, u32[]{:S(2)}) async-start(bf16[32,72,128]{2,1,0:T(8,128)(2,1)} %bitcast.36), calls=%async_computation.1 | async-start | bytes 1179648 | tf_op jit(solution)/shard_map/all_to_all | solution.py:419
  94.6 26.1 %all-gather.4.cloned.1.call-done = bf16[2816,2048]{1,0:T(8,128)(2,1)} async-done(((bf16[176,2048]{1,0:T(8,128)(2,1)}), bf16[2816,2048]{1,0:T(8,128)(2,1)}) %all-gather.4.cloned.1.call-update) | async-done | bytes 11534352 | tf_op jit(solution)/shard_map/all_gather | solution.py:356
  120.8 3.0 %shard_map.123 = bf16[16,32,2048]{2,1,0:T(8,128)(2,1)} custom-call(bf16[16,176,2048]{2,1,0:T(8,128)(2,1)} %bitcast.51), custom_call_target="tpu_custom_call" | custom-call | bytes 4194304 | tf_op jit(solution)/shard_map/pallas_call | solution.py:425
  123.8 2.8 %collective-permute-start.4 = (bf16[16,32,2048]{2,1,0:T(8,128)(2,1)}, bf16[16,32,2048]{2,1,0:T(8,128)(2,1)S(1)}, u32[]{:S(2)}, u32[]{:S(2)}) collective-permute-start(bf16[16,32,2048]{2,1,0:T(8,128)(2,1)} %shard_map.123), channel_id=1, source_target_pairs={{0,1},{1,0},{2,3},{3,2},{4,5},{5,4},{6,7},{7,6},{8,9},{9,8},{10,11... | collective-permute-start | bytes 6291464 | tf_op jit(solution)/shard_map/ppermute | solution.py:433
  126.6 4.3 %all-to-all-done.1 = bf16[32,72,128]{2,1,0:T(8,128)(2,1)S(1)} async-done(((bf16[32,72,128]{2,1,0:T(8,128)(2,1)}), bf16[32,72,128]{2,1,0:T(8,128)(2,1)S(1)}, u32[]{:S(2)}, u32[]{:S(2)}) %all-to-all-start.1) | async-done | bytes 589856 | tf_op jit(solution)/shard_map/all_to_all | solution.py:419
  130.9 0.8 copy-done.7
  131.7 0.8 copy-done.6
  132.6 10.3 %shard_map.125 = bf16[32,144,128]{2,1,0:T(8,128)(2,1)} custom-call(s32[1]{0:T(128)} %bitcast.core_ref, f32[1,2048]{1,0:T(1,128)} %bitcast.63, bf16[4608,128]{1,0:T(8,128)(2,1)} %bitcast.35.residual_ref, bf16[2304,128]{1,0:T(8,128)(2,1)} %bitcast.54, bf16[16,176,2048]{2,1,0:T(8,128)(2,1)} %bitcast.52, bf16[16,32,2048]{2,1,0:T(8,128)(2,1)} %copy-done.6), custom_call_target="tpu_custom_call" | custom-call | flops 4294967296 | bytes 16777216 | tf_op jit(solution)/shard_map/pallas_call | solution.py:434
  142.9 12.0 %all-to-all-start.2 = ((bf16[32,144,128]{2,1,0:T(8,128)(2,1)}), bf16[32,144,128]{2,1,0:T(8,128)(2,1)S(1)}, u32[]{:S(2)}, u32[]{:S(2)}) async-start(bf16[32,144,128]{2,1,0:T(8,128)(2,1)} %shard_map.125), calls=%async_computation.2 | async-start | bytes 2359296 | tf_op jit(solution)/shard_map/all_to_all | solution.py:453
  154.9 0.0 copy-start.5
  154.9 5.6 %shard_map.124.attended_ref = bf16[128,2048]{1,0:T(8,128)(2,1)} custom-call(s32[1]{0:T(128)} %bitcast.core_ref, bf16[128,2048]{1,0:T(8,128)(2,1)} %bitcast.56, bf16[128,1024]{1,0:T(8,128)(2,1)} %copy-done.3, bf16[16,176,2048]{2,1,0:T(8,128)(2,1)} %bitcast.53, bf16[16,32,2048]{2,1,0:T(8,128)(2,1)} %copy-done.6), custom_call_target="tpu_custom_call" | custom-call | flops 536870912 | bytes 6291456 | tf_op jit(solution)/shard_map/pallas_call | solution.py:457
  160.5 55.6 %all-to-all-done.2 = bf16[32,144,128]{2,1,0:T(8,128)(2,1)S(1)} async-done(((bf16[32,144,128]{2,1,0:T(8,128)(2,1)}), bf16[32,144,128]{2,1,0:T(8,128)(2,1)S(1)}, u32[]{:S(2)}, u32[]{:S(2)}) %all-to-all-start.2) | async-done | bytes 1179680 | tf_op jit(solution)/shard_map/all_to_all | solution.py:453
  216.1 2.5 %shard_map.126 = bf16[128,2048]{1,0:T(8,128)(2,1)} custom-call(s32[2,128]{1,0:T(2,128)S(1)} %copy-done.4, f32[2,128]{1,0:T(2,128)S(1)} %bitcast.50, bf16[128,2048]{1,0:T(8,128)(2,1)} %shard_map.124.attended_ref, bf16[4608,128]{1,0:T(8,128)(2,1)S(1)} %bitcast.45), custom_call_target="tpu_custom_call", output_to_operand_aliasing={{}: (2, {})} | custom-call | flops 301989888 | bytes 3145728 | tf_op jit(solution)/shard_map/pallas_call | solution.py:466
  (22 shorter events, 0.1 us)
Async XLA Ops:
  6.5 114.2 %all-gather.4.cloned.1.call-start = ((), (), s32[]{:S(2)}) async-start(), calls=%async_computation.3 | async-start | bytes 12255232 | tf_op jit(solution)/shard_map/all_gather | solution.py:356
  6.5 20.5 %copy-start.8 = (bf16[1,128,576]{1,2,0:T(8,128)(2,1)S(1)}, bf16[1,128,576]{1,2,0:T(8,128)(2,1)}, u32[]{:S(2)}) copy-start(bf16[1,128,576]{1,2,0:T(8,128)(2,1)} %param.14) | copy-start | bytes 442372
  10.0 35.4 %copy-start = (bf16[512,1024]{1,0:T(8,128)(2,1)S(1)}, bf16[512,1024]{1,0:T(8,128)(2,1)}, u32[]{:S(2)}) copy-start(bf16[512,1024]{1,0:T(8,128)(2,1)} %key_up_ref.1) | copy-start | bytes 3145732
  10.0 35.4 %copy-start.2 = (bf16[1,128,1536]{2,1,0:T(8,128)(2,1)S(1)}, bf16[1,128,1536]{2,1,0:T(8,128)(2,1)}, u32[]{:S(2)}) copy-start(bf16[1,128,1536]{2,1,0:T(8,128)(2,1)} %param.13) | copy-start | bytes 1179652
  10.1 78.3 %all-to-all-start = ((bf16[32,144,128]{2,1,0:T(8,128)(2,1)}), bf16[32,144,128]{2,1,0:T(8,128)(2,1)}, u32[]{:S(2)}, u32[]{:S(2)}) async-start(bf16[32,144,128]{2,1,0:T(8,128)(2,1)} %get-tuple-element.18), calls=%async_computation | async-start | bytes 2359296 | tf_op jit(solution)/shard_map/all_to_all | solution.py:357
  39.1 20.3 %collective-permute-start = (bf16[4,576,128]{2,1,0:T(8,128)(2,1)S(1)}, bf16[4,576,128]{2,1,0:T(8,128)(2,1)S(1)}, u32[]{:S(2)}, u32[]{:S(2)}) collective-permute-start(bf16[4,576,128]{2,1,0:T(8,128)(2,1)S(1)} %bitcast.46), channel_id=1, source_target_pairs={{0,128},{32,160},{64,192},{96,224},{128,256},{160,288},{192,320},{... | collective-permute-start | bytes 1769480 | tf_op jit(solution)/shard_map/ppermute | solution.py:364
  42.3 19.3 %collective-permute-start.2 = (bf16[4,576,128]{2,1,0:T(8,128)(2,1)S(1)}, bf16[4,576,128]{2,1,0:T(8,128)(2,1)S(1)}, u32[]{:S(2)}, u32[]{:S(2)}) collective-permute-start(bf16[4,576,128]{2,1,0:T(8,128)(2,1)S(1)} %bitcast.47), channel_id=1, source_target_pairs={{0,384},{32,416},{64,448},{96,480},{128,0},{160,32},{192,64},{224,... | collective-permute-start | bytes 1769480 | tf_op jit(solution)/shard_map/ppermute | solution.py:364
  59.4 14.2 %collective-permute-start.1 = (bf16[2,576,128]{2,1,0:T(8,128)(2,1)S(1)}, bf16[2,576,128]{2,1,0:T(8,128)(2,1)S(1)}, u32[]{:S(2)}, u32[]{:S(2)}) collective-permute-start(bf16[2,576,128]{2,1,0:T(8,128)(2,1)S(1)} %slice.21), channel_id=1, source_target_pairs={{128,256},{160,288},{192,320},{224,352},{256,384},{288,416},{320,4... | collective-permute-start | bytes 884744 | tf_op jit(solution)/shard_map/ppermute | solution.py:364
  61.6 12.0 %collective-permute-start.3 = (bf16[2,576,128]{2,1,0:T(8,128)(2,1)S(1)}, bf16[2,576,128]{2,1,0:T(8,128)(2,1)S(1)}, u32[]{:S(2)}, u32[]{:S(2)}) collective-permute-start(bf16[2,576,128]{2,1,0:T(8,128)(2,1)S(1)} %slice.22), channel_id=1, source_target_pairs={{0,384},{32,416},{64,448},{96,480},{384,256},{416,288},{448,320},{... | collective-permute-start | bytes 884744 | tf_op jit(solution)/shard_map/ppermute | solution.py:364
  68.9 4.7 %copy-start.1 = (bf16[512,1024]{1,0:T(8,128)(2,1)S(1)}, bf16[512,1024]{1,0:T(8,128)(2,1)}, u32[]{:S(2)}) copy-start(bf16[512,1024]{1,0:T(8,128)(2,1)} %value_up_ref.1) | copy-start | bytes 3145732
  69.0 4.7 %copy-start.4 = (s32[2,128]{1,0:T(2,128)S(1)}, s32[2,128]{1,0:T(2,128)}, u32[]{:S(2)}) copy-start(s32[2,128]{1,0:T(2,128)} %get-tuple-element.17.slots_ref) | copy-start | bytes 3076
  79.1 0.7 copy-start.3
  88.4 42.6 %all-to-all-start.1 = ((bf16[32,72,128]{2,1,0:T(8,128)(2,1)}), bf16[32,72,128]{2,1,0:T(8,128)(2,1)S(1)}, u32[]{:S(2)}, u32[]{:S(2)}) async-start(bf16[32,72,128]{2,1,0:T(8,128)(2,1)} %bitcast.36), calls=%async_computation.1 | async-start | bytes 1179648 | tf_op jit(solution)/shard_map/all_to_all | solution.py:419
  123.8 7.1 %collective-permute-start.4 = (bf16[16,32,2048]{2,1,0:T(8,128)(2,1)}, bf16[16,32,2048]{2,1,0:T(8,128)(2,1)S(1)}, u32[]{:S(2)}, u32[]{:S(2)}) collective-permute-start(bf16[16,32,2048]{2,1,0:T(8,128)(2,1)} %shard_map.123), channel_id=1, source_target_pairs={{0,1},{1,0},{2,3},{3,2},{4,5},{5,4},{6,7},{7,6},{8,9},{9,8},{10,11... | collective-permute-start | bytes 6291464 | tf_op jit(solution)/shard_map/ppermute | solution.py:433
  130.9 0.8 copy-start.7
  130.9 1.6 copy-start.6
  142.9 73.3 %all-to-all-start.2 = ((bf16[32,144,128]{2,1,0:T(8,128)(2,1)}), bf16[32,144,128]{2,1,0:T(8,128)(2,1)S(1)}, u32[]{:S(2)}, u32[]{:S(2)}) async-start(bf16[32,144,128]{2,1,0:T(8,128)(2,1)} %shard_map.125), calls=%async_computation.2 | async-start | bytes 2359296 | tf_op jit(solution)/shard_map/all_to_all | solution.py:453
  154.9 61.3 %copy-start.5 = (f32[1,128,2]{1,2,0:T(2,128)S(1)}, f32[1,128,2]{1,2,0:T(2,128)}, u32[]{:S(2)}) copy-start(f32[1,128,2]{1,2,0:T(2,128)} %param.23) | copy-start | bytes 3076
Sparse Core Ops, SparseCore 0:
  10.4 110.3 all-gather.3

commit v4 on v3

--- a/solution.py
+++ b/solution.py
@@ -238,49 +238,48 @@
     copy.wait()
 
 
+def take_rest(
+    packed_ref, residual_ref, values_ref, gate_ref, up_ref, down_ref, residual_out_ref, values_out_ref, tall, short, sems
+):
+    start = packed_ref.shape[1] - 3 * FF_PAD
+    pairs = [
+        (packed_ref.at[:, start + n * FF_PAD : start + (n + 1) * FF_PAD, :], ref)
+        for n, ref in enumerate((gate_ref, up_ref, down_ref))
+    ]
+    copies = start_all(pairs, sems)
+    load_blocks(residual_ref, tall)
+    unpack(tall, D // LANES, residual_out_ref)
+    load_blocks(values_ref, short)
+    unpack(short, values_out_ref.shape[1] // LANES, values_out_ref)
+    for copy in copies:
+        copy.wait()
+
+
 def project(values, projection):
     flat = projection[...].reshape(D, projection.shape[2])
     return lax.dot_general(values, flat, NT, preferred_element_type=F32)
 
 
 def expert(
-    core_ref, gain_ref, residual_ref, values_ref, packed_ref, other_ref, out_ref,
-    residual_rows, value_rows, projection, gate, up, down, tall, short, residual, values, extra, sems,
-):
-    start = projection.shape[1] // 4
-    pairs = [(values_ref, value_rows), (residual_ref, residual_rows)]
-    pairs += projection_pairs(core_ref, packed_ref, other_ref, projection)
-    pairs += [
-        (packed_ref.at[:, start + n * FF_PAD : start + (n + 1) * FF_PAD, :], buffer)
-        for n, buffer in enumerate((gate, up, down))
-    ]
-    copies = [pltpu.make_async_copy(source, target, sems.at[n]) for n, (source, target) in enumerate(pairs)]
-    for copy in copies[:6]:
-        copy.start()
-    copies[0].wait()
-    copies[6].start()
-    load_blocks(value_rows, short)
-    unpack(short, values.shape[1] // LANES, values)
-    copies[1].wait()
-    load_blocks(residual_rows, tall)
-    unpack(tall, D // LANES, residual)
-    for copy in copies[2:6]:
-        copy.wait()
-    copies[7].start()
-    product = project(values[...], projection)
-    attended = (residual[...].astype(F32) + product).astype(BF16).astype(F32)
+    core_ref, gain_ref, residual_ref, values_ref, own_ref, other_ref, gate_ref, up_ref, down_ref, out_ref,
+    projection, extra,
+):
+    part = own_ref.shape[1]
+    depth = projection.shape[2]
+    for ref, half in ((own_ref, core_ref[0]), (other_ref, 1 - core_ref[0])):
+        for n in range(2):
+            row = pl.multiple_of(half * (2 * part) + n * part, part)
+            projection[:, pl.ds(row, part), :] = ref[:, :, n * depth : (n + 1) * depth]
+    product = project(values_ref[...], projection)
+    attended = (residual_ref[...].astype(F32) + product).astype(BF16).astype(F32)
     scale = lax.rsqrt(jnp.mean(attended * attended, axis=1, keepdims=True) + 1e-06)
     normed = (attended * scale * gain_ref[...]).astype(BF16)
-    units = gate.shape[0] * gate.shape[1]
-    copies[6].wait()
-    copies[8].start()
-    gate_proj = lax.dot_general(normed, gate[...].reshape(units, D), NT, preferred_element_type=F32)
-    copies[7].wait()
-    up_proj = lax.dot_general(normed, up[...].reshape(units, D), NT, preferred_element_type=F32)
+    units = gate_ref.shape[0] * FF_PAD
+    gate_proj = lax.dot_general(normed, gate_ref[...].reshape(units, D), NT, preferred_element_type=F32)
+    up_proj = lax.dot_general(normed, up_ref[...].reshape(units, D), NT, preferred_element_type=F32)
     activation = (gate_proj / (1.0 + jnp.exp(-gate_proj)) * up_proj).astype(BF16)
-    copies[8].wait()
     for j in range(0, D // LANES, 2):
-        columns = down[:, :, j * LANES : (j + 2) * LANES].reshape(units, 2 * LANES)
+        columns = down_ref[:, :, j * LANES : (j + 2) * LANES].reshape(units, 2 * LANES)
         put_pair(j, jnp.dot(activation, columns, preferred_element_type=F32), extra, out_ref)
     out_ref[:, 8 * D // LANES :, :] = extra[...].astype(BF16)
 
@@ -431,25 +430,24 @@
         limit=60,
     )(packed_all)
     other_part = lax.ppermute(own_part, "exp", [(e, e + 1 - 2 * (e % 2)) for e in range(n_exp)])
+    gate, up, down, residual_kept, values_kept = call(
+        take_rest,
+        [pltpu.VMEM((n_ctx, FF_PAD, D), BF16)] * 3
+        + [pltpu.VMEM((rows, D), BF16), pltpu.VMEM((rows, values_width), BF16)],
+        scratch=[tall, short, pltpu.SemaphoreType.DMA((3,))],
+        moved=16 << 20,
+        in_specs=[any_space, vmem(), vmem()],
+        limit=42,
+    )(packed_all, residual_rows.reshape(tall_rows, LANES), values_rows.reshape(short_rows, LANES))
     result = call(
         expert,
         jax.ShapeDtypeStruct((n_exp, tall_rows // n_exp, LANES), BF16),
-        scratch=[pltpu.VMEM((tall_rows, LANES), BF16), pltpu.VMEM((short_rows, LANES), BF16), projection]
-        + [pltpu.VMEM((n_ctx, FF_PAD, D), BF16)] * 3
-        + [tall, short, pltpu.VMEM((rows, D), BF16), pltpu.VMEM((rows, values_width), BF16)]
-        + [extra, pltpu.SemaphoreType.DMA((9,))],
+        scratch=[projection, extra],
         flops=4 << 30,
-        moved=16 << 20,
-        in_specs=[smem, vmem()] + [any_space] * 4,
-        limit=60,
-    )(
-        core,
-        norm_gain.reshape(1, D),
-        residual_rows.reshape(tall_rows, LANES),
-        values_rows.reshape(short_rows, LANES),
-        packed_all,
-        other_part,
-    )
+        moved=8 << 20,
+        in_specs=[smem] + [vmem()] * 8,
+        limit=24,
+    )(core, norm_gain.reshape(1, D), residual_kept, values_kept, own_part, other_part, gate, up, down)
     returned = lax.all_to_all(
         result, "exp", split_axis=0, concat_axis=0, tiled=True
     )

time: 226 us -> 221 us (0.978)
  starting transfers between devices: 49.7 us -> 45.5 us
    pallas_call x0 -> x1, Pallas kernels: none -> 5.2 us  [body(): call(take_rest, [pltpu.VMEM((n_ctx, FF_PAD, D), BF16)] * 3 + [pltpu.VMEM(...]
    pallas_call x1, Pallas kernels: 10.3 us -> 5.84 us  [body(): call(expert, jax.ShapeDtypeStruct((n_exp, tall_rows // n_exp, LANES), BF1...]
    all_to_all x1, starting transfers between devices: 12 us -> 8.15 us  [body(): lax.all_to_all(result, 'exp', split_axis=0, concat_axis=0, tiled=True)]
  transfers between devices with their start and end apart: 9 -> 9, of which waited for: 6 -> 6; matrix products, arithmetic and copies ran while one was open for 0% -> 0% of each run, Pallas kernels for 10% -> 12%
where the time goes in v4:
time: 221 us
  waiting for transfers between devices  110 us (50%)
  starting transfers between devices  45.5 us (21%)
  Pallas kernels  38.2 us (17%)
  between operations  13.7 us (6%)
  blocking collectives  12.2 us (6%)
    all_to_all x1, waiting for transfers between devices, body(): lax.all_to_all(result, 'exp', split_axis=0, concat_axis=0, tiled=True)  55.6 us
    all_gather x1, waiting for transfers between devices, body(): packed_all = lax.all_gather(packed, 'ctx')  26.2 us
    all_to_all x1, starting transfers between devices, body(): lax.all_to_all(residual_out, 'exp', split_axis=0, concat_axis=0, tiled=True)  16.9 us
    ppermute x4, waiting for transfers between devices, send(): return lax.ppermute(array, 'ctx', pairs)  15.3 us
    all_gather x1, blocking collectives, body(): near = lax.all_gather(block, 'ctx', axis_index_groups=rows_of_y)  12.2 us
    ppermute x4, starting transfers between devices, send(): return lax.ppermute(array, 'ctx', pairs)  11.2 us
    all_to_all x1, waiting for transfers between devices, body(): lax.all_to_all(residual_out, 'exp', split_axis=0, concat_axis=0, tiled=True)  8.73 us
    all_to_all x1, starting transfers between devices, body(): lax.all_to_all(result, 'exp', split_axis=0, concat_axis=0, tiled=True)  8.15 us
  transfers between devices with their start and end apart: 9, of which 6 were waited for; matrix products, arithmetic and copies ran while one was open for 0% of the time, Pallas kernels for 12%

profile of v4, /device:TPU:1, one launch (start us, length us, event | category | flops | bytes accessed | tf_op | source)
XLA Modules:
  0.0 220.8 jit_solution(11111342665703443853)
XLA Ops:
  6.5 3.3 %shard_map.118 = (bf16[176,2048]{1,0:T(8,128)(2,1)}, bf16[32,144,128]{2,1,0:T(8,128)(2,1)}, s32[2,128]{1,0:T(2,128)}) custom-call(s32[1]{0:T(128)} %bitcast.core_ref, bf16[1024,128]{1,0:T(8,128)(2,1)} %projection_ref.1, bf16[44,2048]{1,0:T(8,128)(2,1)} %bitcast.58, bf16[44,2048]{1,0:T(8,128)(2,1)} %bitcast.59, bf16[44,2048]{1,0:T(8,128)(2,1)} %bitcast.60, ...), custom_call_target="tpu_custom_call" | custom-call | flops 150994944 | bytes 3145728 | tf_op jit(solution)/shard_map/pallas_call | solution.py:342
  9.9 0.0 all-gather.4.cloned.1.call-update
  9.9 16.9 %all-to-all-start = ((bf16[32,144,128]{2,1,0:T(8,128)(2,1)}), bf16[32,144,128]{2,1,0:T(8,128)(2,1)}, u32[]{:S(2)}, u32[]{:S(2)}) async-start(bf16[32,144,128]{2,1,0:T(8,128)(2,1)} %get-tuple-element.23), calls=%async_computation | async-start | bytes 2359296 | tf_op jit(solution)/shard_map/all_to_all | solution.py:356
  26.9 12.2 %all-gather = bf16[2304,128]{1,0:T(8,128)(2,1)S(1)} all-gather(bf16[576,128]{1,0:T(8,128)(2,1)S(1)} %bitcast.61), channel_id=2, replica_groups={{0,32,64,96},{128,160,192,224},{256,288,320,352},{384,416,448,480},{1,3..., dimensions={0}, use_global_device_ids=true | all-gather | bytes 737280 | tf_op jit(solution)/shard_map/all_gather | solution.py:366
  39.0 3.1 %collective-permute-start = (bf16[4,576,128]{2,1,0:T(8,128)(2,1)S(1)}, bf16[4,576,128]{2,1,0:T(8,128)(2,1)S(1)}, u32[]{:S(2)}, u32[]{:S(2)}) collective-permute-start(bf16[4,576,128]{2,1,0:T(8,128)(2,1)S(1)} %bitcast.47), channel_id=1, source_target_pairs={{0,128},{32,160},{64,192},{96,224},{128,256},{160,288},{192,320},{... | collective-permute-start | bytes 1769480 | tf_op jit(solution)/shard_map/ppermute | solution.py:363
  42.2 2.5 %collective-permute-start.2 = (bf16[4,576,128]{2,1,0:T(8,128)(2,1)S(1)}, bf16[4,576,128]{2,1,0:T(8,128)(2,1)S(1)}, u32[]{:S(2)}, u32[]{:S(2)}) collective-permute-start(bf16[4,576,128]{2,1,0:T(8,128)(2,1)S(1)} %bitcast.48), channel_id=1, source_target_pairs={{0,384},{32,416},{64,448},{96,480},{128,0},{160,32},{192,64},{224,... | collective-permute-start | bytes 1769480 | tf_op jit(solution)/shard_map/ppermute | solution.py:363
  44.8 0.1 stack.67
  44.9 0.1 iota_add_fusion
  45.0 0.5 shard_map.119.absorbed_ref
  45.5 13.8 %collective-permute-done.up_ref = bf16[4,576,128]{2,1,0:T(8,128)(2,1)S(1)} collective-permute-done((bf16[4,576,128]{2,1,0:T(8,128)(2,1)S(1)}, bf16[4,576,128]{2,1,0:T(8,128)(2,1)S(1)}, u32[]{:S(2)}, u32[]{:S(2)}) %collective-permute-start) | collective-permute-done | bytes 589856 | tf_op jit(solution)/shard_map/ppermute | solution.py:363
  59.3 0.7 collective-permute-start.1
  60.0 1.4 collective-permute-done.2.down_ref
  61.5 4.9 %collective-permute-start.3 = (bf16[2,576,128]{2,1,0:T(8,128)(2,1)S(1)}, bf16[2,576,128]{2,1,0:T(8,128)(2,1)S(1)}, u32[]{:S(2)}, u32[]{:S(2)}) collective-permute-start(bf16[2,576,128]{2,1,0:T(8,128)(2,1)S(1)} %slice.22), channel_id=1, source_target_pairs={{0,384},{32,416},{64,448},{96,480},{384,256},{416,288},{448,320},{... | collective-permute-start | bytes 884744 | tf_op jit(solution)/shard_map/ppermute | solution.py:363
  66.4 2.3 %shard_map.120 = (f32[1024,512]{1,0:T(8,128)S(1)}, f32[1024,2]{1,0:T(8,128)S(1)}) custom-call(s32[1]{0:T(128)} %bitcast.11.place_ref, s32[1,512]{1,0:T(1,128)S(1)} %get-tuple-element.39.key_at_ref, bf16[4,576,128]{2,1,0:T(8,128)(2,1)S(1)} %bitcast.49, bf16[1024,576]{1,0:T(8,128)(2,1)S(1)} %shard_map.119.absorbed_ref), custom_call_target="tpu_custom_call" | custom-call | flops 1073741824 | bytes 6291456 | tf_op jit(solution)/shard_map/pallas_call | solution.py:388
  68.7 0.0 copy-start.3
  68.7 0.0 copy-start.7
  68.7 4.6 %shard_map.121 = (f32[1024,512]{1,0:T(8,128)S(1)}, f32[1024,2]{1,0:T(8,128)S(1)}) custom-call(s32[1]{0:T(128)} %bitcast.11.place_ref, s32[1,1024]{1,0:T(1,128)S(1)} %slice.23.key_at_ref, bf16[4,576,128]{2,1,0:T(8,128)(2,1)S(1)} %collective-permute-done.up_ref, bf16[4,576,128]{2,1,0:T(8,128)(2,1)S(1)} %collective-permute-done.2.down_ref, ...), custom_call_target="tpu_custom_call" | custom-call | flops 2147483648 | bytes 6291456 | tf_op jit(solution)/shard_map/pallas_call | solution.py:396
  73.3 5.5 %shard_map.122 = (bf16[128,1024]{1,0:T(8,128)(2,1)S(1)}, bf16[2304,128]{1,0:T(8,128)(2,1)}) custom-call(s32[1]{0:T(128)} %bitcast.11.place_ref, s32[2,128]{1,0:T(2,128)S(1)} %copy-done.7, s32[1,512]{1,0:T(1,128)S(1)} %get-tuple-element.40.key_at_ref, bf16[2,576,128]{2,1,0:T(8,128)(2,1)S(1)} %collective-permute-done.1.up_ref, ...), custom_call_target="tpu_custom_call" | custom-call | flops 1073741824 | bytes 6291456 | tf_op jit(solution)/shard_map/pallas_call | solution.py:405
  78.8 0.7 copy-done.5
  79.5 8.7 %all-to-all-done = bf16[32,144,128]{2,1,0:T(8,128)(2,1)} async-done(((bf16[32,144,128]{2,1,0:T(8,128)(2,1)}), bf16[32,144,128]{2,1,0:T(8,128)(2,1)}, u32[]{:S(2)}, u32[]{:S(2)}) %all-to-all-start) | async-done | bytes 1179680 | tf_op jit(solution)/shard_map/all_to_all | solution.py:356
  88.2 6.4 %all-to-all-start.1 = ((bf16[32,72,128]{2,1,0:T(8,128)(2,1)}), bf16[32,72,128]{2,1,0:T(8,128)(2,1)S(1)}, u32[]{:S(2)}, u32[]{:S(2)}) async-start(bf16[32,72,128]{2,1,0:T(8,128)(2,1)} %bitcast.36), calls=%async_computation.1 | async-start | bytes 1179648 | tf_op jit(solution)/shard_map/all_to_all | solution.py:418
  94.6 26.2 %all-gather.4.cloned.1.call-done = bf16[2816,2048]{1,0:T(8,128)(2,1)} async-done(((bf16[176,2048]{1,0:T(8,128)(2,1)}), bf16[2816,2048]{1,0:T(8,128)(2,1)}) %all-gather.4.cloned.1.call-update) | async-done | bytes 11534352 | tf_op jit(solution)/shard_map/all_gather | solution.py:355
  120.8 2.9 %shard_map.123.own_ref = bf16[16,32,2048]{2,1,0:T(8,128)(2,1)} custom-call(bf16[16,176,2048]{2,1,0:T(8,128)(2,1)} %bitcast.53), custom_call_target="tpu_custom_call" | custom-call | bytes 4194304 | tf_op jit(solution)/shard_map/pallas_call | solution.py:424
  123.8 2.8 %collective-permute-start.4 = (bf16[16,32,2048]{2,1,0:T(8,128)(2,1)}, bf16[16,32,2048]{2,1,0:T(8,128)(2,1)S(1)}, u32[]{:S(2)}, u32[]{:S(2)}) collective-permute-start(bf16[16,32,2048]{2,1,0:T(8,128)(2,1)} %shard_map.123.own_ref), channel_id=1, source_target_pairs={{0,1},{1,0},{2,3},{3,2},{4,5},{5,4},{6,7},{7,6},{8,9},{9,8},{10,11... | collective-permute-start | bytes 6291464 | tf_op jit(solution)/shard_map/ppermute | solution.py:432
  126.5 4.3 %all-to-all-done.1 = bf16[32,72,128]{2,1,0:T(8,128)(2,1)S(1)} async-done(((bf16[32,72,128]{2,1,0:T(8,128)(2,1)}), bf16[32,72,128]{2,1,0:T(8,128)(2,1)S(1)}, u32[]{:S(2)}, u32[]{:S(2)}) %all-to-all-start.1) | async-done | bytes 589856 | tf_op jit(solution)/shard_map/all_to_all | solution.py:418
  130.9 5.2 %shard_map.125 = (bf16[16,48,2048]{2,1,0:T(8,128)(2,1)S(1)}, bf16[16,48,2048]{2,1,0:T(8,128)(2,1)S(1)}, bf16[16,48,2048]{2,1,0:T(8,128)(2,1)S(1)}, bf16[288,2048]{1,0:T(8,128)(2,1)S(1)}, bf16[288,1024]{1,0:T(8,128)(2,1)S(1)}) custom-call(bf16[16,176,2048]{2,1,0:T(8,128)(2,1)} %bitcast.54, bf16[4608,128]{1,0:T(8,128)(2,1)} %bitcast.35.residual_ref, ...), custom_call_target="tpu_custom_call" | custom-call | bytes 16777216 | tf_op jit(solution)/shard_map/pallas_call | solution.py:433
  136.1 5.8 %shard_map.126 = bf16[32,144,128]{2,1,0:T(8,128)(2,1)} custom-call(s32[1]{0:T(128)} %bitcast.core_ref, f32[1,2048]{1,0:T(1,128)S(1)} %bitcast.51, bf16[288,2048]{1,0:T(8,128)(2,1)S(1)} %get-tuple-element.34.residual_ref, bf16[288,1024]{1,0:T(8,128)(2,1)S(1)} %get-tuple-element.35.values_ref, bf16[16,32,2048]{2,1,0:T(8,128)(2,1)S(1)} %copy-done.1, ...), custom_call_target="tpu_custom_call" | custom-call | flops 4294967296 | bytes 8388608 | tf_op jit(solution)/shard_map/pallas_call | solution.py:442
  142.0 8.1 %all-to-all-start.2 = ((bf16[32,144,128]{2,1,0:T(8,128)(2,1)}), bf16[32,144,128]{2,1,0:T(8,128)(2,1)S(1)}, u32[]{:S(2)}, u32[]{:S(2)}) async-start(bf16[32,144,128]{2,1,0:T(8,128)(2,1)} %shard_map.126), calls=%async_computation.2 | async-start | bytes 2359296 | tf_op jit(solution)/shard_map/all_to_all | solution.py:451
  150.1 0.0 copy-start.8
  150.1 5.6 %shard_map.124.attended_ref = bf16[128,2048]{1,0:T(8,128)(2,1)} custom-call(s32[1]{0:T(128)} %bitcast.core_ref, bf16[128,2048]{1,0:T(8,128)(2,1)} %bitcast.57, bf16[128,1024]{1,0:T(8,128)(2,1)} %copy-done.5, bf16[16,176,2048]{2,1,0:T(8,128)(2,1)} %bitcast.55, bf16[16,32,2048]{2,1,0:T(8,128)(2,1)} %copy-done), custom_call_target="tpu_custom_call" | custom-call | flops 536870912 | bytes 6291456 | tf_op jit(solution)/shard_map/pallas_call | solution.py:455
  155.8 55.6 %all-to-all-done.2 = bf16[32,144,128]{2,1,0:T(8,128)(2,1)S(1)} async-done(((bf16[32,144,128]{2,1,0:T(8,128)(2,1)}), bf16[32,144,128]{2,1,0:T(8,128)(2,1)S(1)}, u32[]{:S(2)}, u32[]{:S(2)}) %all-to-all-start.2) | async-done | bytes 1179680 | tf_op jit(solution)/shard_map/all_to_all | solution.py:451
  211.4 2.5 %shard_map.127 = bf16[128,2048]{1,0:T(8,128)(2,1)} custom-call(s32[2,128]{1,0:T(2,128)S(1)} %copy-done.7, f32[2,128]{1,0:T(2,128)S(1)} %bitcast.52, bf16[128,2048]{1,0:T(8,128)(2,1)} %shard_map.124.attended_ref, bf16[4608,128]{1,0:T(8,128)(2,1)S(1)} %bitcast.45), custom_call_target="tpu_custom_call", output_to_operand_aliasing={{}: (2, {})} | custom-call | flops 301989888 | bytes 3145728 | tf_op jit(solution)/shard_map/pallas_call | solution.py:464
  (25 shorter events, 0.1 us)
Async XLA Ops:
  6.5 114.3 %all-gather.4.cloned.1.call-start = ((), (), s32[]{:S(2)}) async-start(), calls=%async_computation.3 | async-start | bytes 12255232 | tf_op jit(solution)/shard_map/all_gather | solution.py:355
  6.5 20.3 %copy-start.9 = (bf16[1,128,576]{1,2,0:T(8,128)(2,1)S(1)}, bf16[1,128,576]{1,2,0:T(8,128)(2,1)}, u32[]{:S(2)}) copy-start(bf16[1,128,576]{1,2,0:T(8,128)(2,1)} %param.14) | copy-start | bytes 442372
  9.9 35.1 %copy-start.2 = (bf16[512,1024]{1,0:T(8,128)(2,1)S(1)}, bf16[512,1024]{1,0:T(8,128)(2,1)}, u32[]{:S(2)}) copy-start(bf16[512,1024]{1,0:T(8,128)(2,1)} %key_up_ref.1) | copy-start | bytes 3145732
  9.9 35.1 %copy-start.4 = (bf16[1,128,1536]{2,1,0:T(8,128)(2,1)S(1)}, bf16[1,128,1536]{2,1,0:T(8,128)(2,1)}, u32[]{:S(2)}) copy-start(bf16[1,128,1536]{2,1,0:T(8,128)(2,1)} %param.13) | copy-start | bytes 1179652
  9.9 78.3 %all-to-all-start = ((bf16[32,144,128]{2,1,0:T(8,128)(2,1)}), bf16[32,144,128]{2,1,0:T(8,128)(2,1)}, u32[]{:S(2)}, u32[]{:S(2)}) async-start(bf16[32,144,128]{2,1,0:T(8,128)(2,1)} %get-tuple-element.23), calls=%async_computation | async-start | bytes 2359296 | tf_op jit(solution)/shard_map/all_to_all | solution.py:356
  39.0 20.3 %collective-permute-start = (bf16[4,576,128]{2,1,0:T(8,128)(2,1)S(1)}, bf16[4,576,128]{2,1,0:T(8,128)(2,1)S(1)}, u32[]{:S(2)}, u32[]{:S(2)}) collective-permute-start(bf16[4,576,128]{2,1,0:T(8,128)(2,1)S(1)} %bitcast.47), channel_id=1, source_target_pairs={{0,128},{32,160},{64,192},{96,224},{128,256},{160,288},{192,320},{... | collective-permute-start | bytes 1769480 | tf_op jit(solution)/shard_map/ppermute | solution.py:363
  42.2 19.3 %collective-permute-start.2 = (bf16[4,576,128]{2,1,0:T(8,128)(2,1)S(1)}, bf16[4,576,128]{2,1,0:T(8,128)(2,1)S(1)}, u32[]{:S(2)}, u32[]{:S(2)}) collective-permute-start(bf16[4,576,128]{2,1,0:T(8,128)(2,1)S(1)} %bitcast.48), channel_id=1, source_target_pairs={{0,384},{32,416},{64,448},{96,480},{128,0},{160,32},{192,64},{224,... | collective-permute-start | bytes 1769480 | tf_op jit(solution)/shard_map/ppermute | solution.py:363
  59.3 13.9 %collective-permute-start.1 = (bf16[2,576,128]{2,1,0:T(8,128)(2,1)S(1)}, bf16[2,576,128]{2,1,0:T(8,128)(2,1)S(1)}, u32[]{:S(2)}, u32[]{:S(2)}) collective-permute-start(bf16[2,576,128]{2,1,0:T(8,128)(2,1)S(1)} %slice.21), channel_id=1, source_target_pairs={{128,256},{160,288},{192,320},{224,352},{256,384},{288,416},{320,4... | collective-permute-start | bytes 884744 | tf_op jit(solution)/shard_map/ppermute | solution.py:363
  61.5 11.8 %collective-permute-start.3 = (bf16[2,576,128]{2,1,0:T(8,128)(2,1)S(1)}, bf16[2,576,128]{2,1,0:T(8,128)(2,1)S(1)}, u32[]{:S(2)}, u32[]{:S(2)}) collective-permute-start(bf16[2,576,128]{2,1,0:T(8,128)(2,1)S(1)} %slice.22), channel_id=1, source_target_pairs={{0,384},{32,416},{64,448},{96,480},{384,256},{416,288},{448,320},{... | collective-permute-start | bytes 884744 | tf_op jit(solution)/shard_map/ppermute | solution.py:363
  68.7 4.6 %copy-start.3 = (bf16[512,1024]{1,0:T(8,128)(2,1)S(1)}, bf16[512,1024]{1,0:T(8,128)(2,1)}, u32[]{:S(2)}) copy-start(bf16[512,1024]{1,0:T(8,128)(2,1)} %value_up_ref.1) | copy-start | bytes 3145732
  68.7 4.6 %copy-start.7 = (s32[2,128]{1,0:T(2,128)S(1)}, s32[2,128]{1,0:T(2,128)}, u32[]{:S(2)}) copy-start(s32[2,128]{1,0:T(2,128)} %get-tuple-element.22.slots_ref) | copy-start | bytes 3076
  78.8 0.7 copy-start.5
  88.2 42.7 %all-to-all-start.1 = ((bf16[32,72,128]{2,1,0:T(8,128)(2,1)}), bf16[32,72,128]{2,1,0:T(8,128)(2,1)S(1)}, u32[]{:S(2)}, u32[]{:S(2)}) async-start(bf16[32,72,128]{2,1,0:T(8,128)(2,1)} %bitcast.36), calls=%async_computation.1 | async-start | bytes 1179648 | tf_op jit(solution)/shard_map/all_to_all | solution.py:418
  123.8 12.3 %collective-permute-start.4 = (bf16[16,32,2048]{2,1,0:T(8,128)(2,1)}, bf16[16,32,2048]{2,1,0:T(8,128)(2,1)S(1)}, u32[]{:S(2)}, u32[]{:S(2)}) collective-permute-start(bf16[16,32,2048]{2,1,0:T(8,128)(2,1)} %shard_map.123.own_ref), channel_id=1, source_target_pairs={{0,1},{1,0},{2,3},{3,2},{4,5},{5,4},{6,7},{7,6},{8,9},{9,8},{10,11... | collective-permute-start | bytes 6291464 | tf_op jit(solution)/shard_map/ppermute | solution.py:432
  130.9 5.2 %copy-start.1 = (bf16[16,32,2048]{2,1,0:T(8,128)(2,1)S(1)}, bf16[16,32,2048]{2,1,0:T(8,128)(2,1)}, u32[]{:S(2)}) copy-start(bf16[16,32,2048]{2,1,0:T(8,128)(2,1)} %shard_map.123.own_ref) | copy-start | bytes 6291460
  130.9 5.2 %copy-start.6 = (f32[2048]{0:T(1024)S(1)}, f32[2048]{0:T(1024)}, u32[]{:S(2)}) copy-start(f32[2048]{0:T(1024)} %param.18) | copy-start | bytes 24580
  136.1 5.9 %copy-start = (bf16[16,32,2048]{2,1,0:T(8,128)(2,1)}, bf16[16,32,2048]{2,1,0:T(8,128)(2,1)S(1)}, u32[]{:S(2)}) copy-start(bf16[16,32,2048]{2,1,0:T(8,128)(2,1)S(1)} %collective-permute-done.4.other_ref) | copy-start | bytes 6291460
  142.0 69.4 %all-to-all-start.2 = ((bf16[32,144,128]{2,1,0:T(8,128)(2,1)}), bf16[32,144,128]{2,1,0:T(8,128)(2,1)S(1)}, u32[]{:S(2)}, u32[]{:S(2)}) async-start(bf16[32,144,128]{2,1,0:T(8,128)(2,1)} %shard_map.126), calls=%async_computation.2 | async-start | bytes 2359296 | tf_op jit(solution)/shard_map/all_to_all | solution.py:451
  150.1 61.3 %copy-start.8 = (f32[1,128,2]{1,2,0:T(2,128)S(1)}, f32[1,128,2]{1,2,0:T(2,128)}, u32[]{:S(2)}) copy-start(f32[1,128,2]{1,2,0:T(2,128)} %param.23) | copy-start | bytes 3076
Sparse Core Ops, SparseCore 0:
  10.4 110.3 all-gather.3

commit v5 on v4

--- a/solution.py
+++ b/solution.py
@@ -239,12 +239,12 @@
 
 
 def take_rest(
-    packed_ref, residual_ref, values_ref, gate_ref, up_ref, down_ref, residual_out_ref, values_out_ref, tall, short, sems
+    packed_ref, residual_ref, values_ref, gate_ref, up_ref, residual_out_ref, values_out_ref, tall, short, sems
 ):
     start = packed_ref.shape[1] - 3 * FF_PAD
     pairs = [
         (packed_ref.at[:, start + n * FF_PAD : start + (n + 1) * FF_PAD, :], ref)
-        for n, ref in enumerate((gate_ref, up_ref, down_ref))
+        for n, ref in enumerate((gate_ref, up_ref))
     ]
     copies = start_all(pairs, sems)
     load_blocks(residual_ref, tall)
@@ -261,9 +261,12 @@
 
 
 def expert(
-    core_ref, gain_ref, residual_ref, values_ref, own_ref, other_ref, gate_ref, up_ref, down_ref, out_ref,
-    projection, extra,
+    core_ref, gain_ref, residual_ref, values_ref, own_ref, other_ref, gate_ref, up_ref, packed_ref, out_ref,
+    projection, extra, down, sem,
 ):
+    start = packed_ref.shape[1] - FF_PAD
+    copy = pltpu.make_async_copy(packed_ref.at[:, start : start + FF_PAD, :], down, sem)
+    copy.start()
     part = own_ref.shape[1]
     depth = projection.shape[2]
     for ref, half in ((own_ref, core_ref[0]), (other_ref, 1 - core_ref[0])):
@@ -278,8 +281,9 @@
     gate_proj = lax.dot_general(normed, gate_ref[...].reshape(units, D), NT, preferred_element_type=F32)
     up_proj = lax.dot_general(normed, up_ref[...].reshape(units, D), NT, preferred_element_type=F32)
     activation = (gate_proj / (1.0 + jnp.exp(-gate_proj)) * up_proj).astype(BF16)
+    copy.wait()
     for j in range(0, D // LANES, 2):
-        columns = down_ref[:, :, j * LANES : (j + 2) * LANES].reshape(units, 2 * LANES)
+        columns = down[:, :, j * LANES : (j + 2) * LANES].reshape(units, 2 * LANES)
         put_pair(j, jnp.dot(activation, columns, preferred_element_type=F32), extra, out_ref)
     out_ref[:, 8 * D // LANES :, :] = extra[...].astype(BF16)
 
@@ -430,24 +434,24 @@
         limit=60,
     )(packed_all)
     other_part = lax.ppermute(own_part, "exp", [(e, e + 1 - 2 * (e % 2)) for e in range(n_exp)])
-    gate, up, down, residual_kept, values_kept = call(
+    gate, up, residual_kept, values_kept = call(
         take_rest,
-        [pltpu.VMEM((n_ctx, FF_PAD, D), BF16)] * 3
+        [pltpu.VMEM((n_ctx, FF_PAD, D), BF16)] * 2
         + [pltpu.VMEM((rows, D), BF16), pltpu.VMEM((rows, values_width), BF16)],
-        scratch=[tall, short, pltpu.SemaphoreType.DMA((3,))],
+        scratch=[tall, short, pltpu.SemaphoreType.DMA((2,))],
         moved=16 << 20,
         in_specs=[any_space, vmem(), vmem()],
-        limit=42,
+        limit=46,
     )(packed_all, residual_rows.reshape(tall_rows, LANES), values_rows.reshape(short_rows, LANES))
     result = call(
         expert,
         jax.ShapeDtypeStruct((n_exp, tall_rows // n_exp, LANES), BF16),
-        scratch=[projection, extra],
+        scratch=[projection, extra, pltpu.VMEM((n_ctx, FF_PAD, D), BF16), pltpu.SemaphoreType.DMA],
         flops=4 << 30,
         moved=8 << 20,
-        in_specs=[smem] + [vmem()] * 8,
-        limit=24,
-    )(core, norm_gain.reshape(1, D), residual_kept, values_kept, own_part, other_part, gate, up, down)
+        in_specs=[smem] + [vmem()] * 7 + [any_space],
+        limit=46,
+    )(core, norm_gain.reshape(1, D), residual_kept, values_kept, own_part, other_part, gate, up, packed_all)
     returned = lax.all_to_all(
         result, "exp", split_axis=0, concat_axis=0, tiled=True
     )

time: 221 us -> 229 us (1.036)
  local copies, waits for them, and re-layouts: 0.88 us -> 5.06 us
  Pallas kernels: 38.2 us -> 41.2 us
    unnamed x20 -> x26, local copies, waits for them, and re-layouts: 0.74 us -> 4.92 us
    pallas_call x1, Pallas kernels: 5.84 us -> 9.6 us  [body(): call(expert, jax.ShapeDtypeStruct((n_exp, tall_rows // n_exp, LANES), BF1...]
  transfers between devices with their start and end apart: 9 -> 9, of which waited for: 6 -> 6; matrix products, arithmetic and copies ran while one was open for 0% -> 0% of each run, Pallas kernels for 12% -> 11%
where the time goes in v5:
time: 229 us; the launch traced here: 228 us
  waiting for transfers between devices  110 us (48%)
  starting transfers between devices  45.5 us (20%)
  Pallas kernels  41.2 us (18%)
  between operations  13.7 us (6%)
  blocking collectives  12.2 us (5%)
  local copies, waits for them, and re-layouts  5.06 us (2%)
    all_to_all x1, waiting for transfers between devices, body(): lax.all_to_all(result, 'exp', split_axis=0, concat_axis=0, tiled=True)  55.6 us
    all_gather x1, waiting for transfers between devices, body(): packed_all = lax.all_gather(packed, 'ctx')  26.1 us
    all_to_all x1, starting transfers between devices, body(): lax.all_to_all(residual_out, 'exp', split_axis=0, concat_axis=0, tiled=True)  16.9 us
    ppermute x4, waiting for transfers between devices, send(): return lax.ppermute(array, 'ctx', pairs)  15.3 us
    all_gather x1, blocking collectives, body(): near = lax.all_gather(block, 'ctx', axis_index_groups=rows_of_y)  12.2 us
    ppermute x4, starting transfers between devices, send(): return lax.ppermute(array, 'ctx', pairs)  11.3 us
    pallas_call x1, Pallas kernels, body(): call(expert, jax.ShapeDtypeStruct((n_exp, tall_rows // n_exp, LANES), BF1...  9.6 us
    all_to_all x1, waiting for transfers between devices, body(): lax.all_to_all(residual_out, 'exp', split_axis=0, concat_axis=0, tiled=True)  8.62 us
  transfers between devices with their start and end apart: 9, of which 6 were waited for; matrix products, arithmetic and copies ran while one was open for 0% of the time, Pallas kernels for 11%

profile of v5, /device:TPU:1, one launch (start us, length us, event | category | flops | bytes accessed | tf_op | source)
XLA Modules:
  0.0 227.9 jit_solution(461945116889685467)
XLA Ops:
  6.5 3.3 %shard_map.118 = (bf16[176,2048]{1,0:T(8,128)(2,1)}, bf16[32,144,128]{2,1,0:T(8,128)(2,1)}, s32[2,128]{1,0:T(2,128)}) custom-call(s32[1]{0:T(128)} %bitcast.core_ref, bf16[1024,128]{1,0:T(8,128)(2,1)} %projection_ref.1, bf16[44,2048]{1,0:T(8,128)(2,1)} %bitcast.59, bf16[44,2048]{1,0:T(8,128)(2,1)} %bitcast.60, bf16[44,2048]{1,0:T(8,128)(2,1)} %bitcast.61, ...), custom_call_target="tpu_custom_call" | custom-call | flops 150994944 | bytes 3145728 | tf_op jit(solution)/shard_map/pallas_call | solution.py:346
  9.9 0.0 all-gather.4.cloned.1.call-update
  9.9 16.9 %all-to-all-start = ((bf16[32,144,128]{2,1,0:T(8,128)(2,1)}), bf16[32,144,128]{2,1,0:T(8,128)(2,1)}, u32[]{:S(2)}, u32[]{:S(2)}) async-start(bf16[32,144,128]{2,1,0:T(8,128)(2,1)} %get-tuple-element.22), calls=%async_computation | async-start | bytes 2359296 | tf_op jit(solution)/shard_map/all_to_all | solution.py:360
  26.9 12.2 %all-gather = bf16[2304,128]{1,0:T(8,128)(2,1)S(1)} all-gather(bf16[576,128]{1,0:T(8,128)(2,1)S(1)} %bitcast.62), channel_id=2, replica_groups={{0,32,64,96},{128,160,192,224},{256,288,320,352},{384,416,448,480},{1,3..., dimensions={0}, use_global_device_ids=true | all-gather | bytes 737280 | tf_op jit(solution)/shard_map/all_gather | solution.py:370
  39.0 3.1 %collective-permute-start = (bf16[4,576,128]{2,1,0:T(8,128)(2,1)S(1)}, bf16[4,576,128]{2,1,0:T(8,128)(2,1)S(1)}, u32[]{:S(2)}, u32[]{:S(2)}) collective-permute-start(bf16[4,576,128]{2,1,0:T(8,128)(2,1)S(1)} %bitcast.46), channel_id=1, source_target_pairs={{0,128},{32,160},{64,192},{96,224},{128,256},{160,288},{192,320},{... | collective-permute-start | bytes 1769480 | tf_op jit(solution)/shard_map/ppermute | solution.py:367
  42.2 2.5 %collective-permute-start.2 = (bf16[4,576,128]{2,1,0:T(8,128)(2,1)S(1)}, bf16[4,576,128]{2,1,0:T(8,128)(2,1)S(1)}, u32[]{:S(2)}, u32[]{:S(2)}) collective-permute-start(bf16[4,576,128]{2,1,0:T(8,128)(2,1)S(1)} %bitcast.47), channel_id=1, source_target_pairs={{0,384},{32,416},{64,448},{96,480},{128,0},{160,32},{192,64},{224,... | collective-permute-start | bytes 1769480 | tf_op jit(solution)/shard_map/ppermute | solution.py:367
  44.8 0.1 stack.67
  44.9 0.1 iota_add_fusion
  45.0 0.5 shard_map.119.absorbed_ref
  45.5 13.8 %collective-permute-done.up_ref = bf16[4,576,128]{2,1,0:T(8,128)(2,1)S(1)} collective-permute-done((bf16[4,576,128]{2,1,0:T(8,128)(2,1)S(1)}, bf16[4,576,128]{2,1,0:T(8,128)(2,1)S(1)}, u32[]{:S(2)}, u32[]{:S(2)}) %collective-permute-start) | collective-permute-done | bytes 589856 | tf_op jit(solution)/shard_map/ppermute | solution.py:367
  59.3 0.7 collective-permute-start.1
  60.0 1.4 collective-permute-done.2.down_ref
  61.5 5.0 %collective-permute-start.3 = (bf16[2,576,128]{2,1,0:T(8,128)(2,1)S(1)}, bf16[2,576,128]{2,1,0:T(8,128)(2,1)S(1)}, u32[]{:S(2)}, u32[]{:S(2)}) collective-permute-start(bf16[2,576,128]{2,1,0:T(8,128)(2,1)S(1)} %slice.22), channel_id=1, source_target_pairs={{0,384},{32,416},{64,448},{96,480},{384,256},{416,288},{448,320},{... | collective-permute-start | bytes 884744 | tf_op jit(solution)/shard_map/ppermute | solution.py:367
  66.4 2.3 shard_map.120
  68.7 4.6 %shard_map.121 = (f32[1024,512]{1,0:T(8,128)S(1)}, f32[1024,2]{1,0:T(8,128)S(1)}) custom-call(s32[1]{0:T(128)} %bitcast.11.place_ref, s32[1,1024]{1,0:T(1,128)S(1)} %slice.23.key_at_ref, bf16[4,576,128]{2,1,0:T(8,128)(2,1)S(1)} %collective-permute-done.up_ref, bf16[4,576,128]{2,1,0:T(8,128)(2,1)S(1)} %collective-permute-done.2.down_ref, ...), custom_call_target="tpu_custom_call" | custom-call | flops 2147483648 | bytes 6291456 | tf_op jit(solution)/shard_map/pallas_call | solution.py:400
  73.4 5.5 %shard_map.122 = (bf16[128,1024]{1,0:T(8,128)(2,1)S(1)}, bf16[2304,128]{1,0:T(8,128)(2,1)}) custom-call(s32[1]{0:T(128)} %bitcast.11.place_ref, s32[2,128]{1,0:T(2,128)S(1)} %copy-done.9, s32[1,512]{1,0:T(1,128)S(1)} %get-tuple-element.38.key_at_ref, bf16[2,576,128]{2,1,0:T(8,128)(2,1)S(1)} %collective-permute-done.1.up_ref, ...), custom_call_target="tpu_custom_call" | custom-call | flops 1073741824 | bytes 6291456 | tf_op jit(solution)/shard_map/pallas_call | solution.py:409
  78.9 0.7 copy-done.7
  79.6 8.6 %all-to-all-done = bf16[32,144,128]{2,1,0:T(8,128)(2,1)} async-done(((bf16[32,144,128]{2,1,0:T(8,128)(2,1)}), bf16[32,144,128]{2,1,0:T(8,128)(2,1)}, u32[]{:S(2)}, u32[]{:S(2)}) %all-to-all-start) | async-done | bytes 1179680 | tf_op jit(solution)/shard_map/all_to_all | solution.py:360
  88.2 6.5 %all-to-all-start.1 = ((bf16[32,72,128]{2,1,0:T(8,128)(2,1)}), bf16[32,72,128]{2,1,0:T(8,128)(2,1)S(1)}, u32[]{:S(2)}, u32[]{:S(2)}) async-start(bf16[32,72,128]{2,1,0:T(8,128)(2,1)} %bitcast.36), calls=%async_computation.1 | async-start | bytes 1179648 | tf_op jit(solution)/shard_map/all_to_all | solution.py:422
  94.7 26.1 %all-gather.4.cloned.1.call-done = bf16[2816,2048]{1,0:T(8,128)(2,1)} async-done(((bf16[176,2048]{1,0:T(8,128)(2,1)}), bf16[2816,2048]{1,0:T(8,128)(2,1)}) %all-gather.4.cloned.1.call-update) | async-done | bytes 11534352 | tf_op jit(solution)/shard_map/all_gather | solution.py:359
  120.8 2.9 %shard_map.123.own_ref = bf16[16,32,2048]{2,1,0:T(8,128)(2,1)} custom-call(bf16[16,176,2048]{2,1,0:T(8,128)(2,1)} %bitcast.52), custom_call_target="tpu_custom_call" | custom-call | bytes 4194304 | tf_op jit(solution)/shard_map/pallas_call | solution.py:428
  123.7 2.8 %collective-permute-start.4 = (bf16[16,32,2048]{2,1,0:T(8,128)(2,1)}, bf16[16,32,2048]{2,1,0:T(8,128)(2,1)S(1)}, u32[]{:S(2)}, u32[]{:S(2)}) collective-permute-start(bf16[16,32,2048]{2,1,0:T(8,128)(2,1)} %shard_map.123.own_ref), channel_id=1, source_target_pairs={{0,1},{1,0},{2,3},{3,2},{4,5},{5,4},{6,7},{7,6},{8,9},{9,8},{10,11... | collective-permute-start | bytes 6291464 | tf_op jit(solution)/shard_map/ppermute | solution.py:436
  126.5 4.5 %all-to-all-done.1 = bf16[32,72,128]{2,1,0:T(8,128)(2,1)S(1)} async-done(((bf16[32,72,128]{2,1,0:T(8,128)(2,1)}), bf16[32,72,128]{2,1,0:T(8,128)(2,1)S(1)}, u32[]{:S(2)}, u32[]{:S(2)}) %all-to-all-start.1) | async-done | bytes 589856 | tf_op jit(solution)/shard_map/all_to_all | solution.py:422
  131.0 0.9 copy-done.11
  131.8 4.4 %shard_map.125 = (bf16[16,48,2048]{2,1,0:T(8,128)(2,1)S(1)}, bf16[16,48,2048]{2,1,0:T(8,128)(2,1)S(1)}, bf16[288,2048]{1,0:T(8,128)(2,1)S(1)}, bf16[288,1024]{1,0:T(8,128)(2,1)S(1)}) custom-call(bf16[16,176,2048]{2,1,0:T(8,128)(2,1)} %bitcast.53, bf16[4608,128]{1,0:T(8,128)(2,1)} %bitcast.35.residual_ref, bf16[2304,128]{1,0:T(8,128)(2,1)} %bitcast.56), custom_call_target="tpu_custom_call" | custom-call | bytes 16777216 | tf_op jit(solution)/shard_map/pallas_call | solution.py:437
  136.3 1.7 copy-done.2
  138.0 1.6 copy-done.3
  139.6 9.6 %shard_map.126 = bf16[32,144,128]{2,1,0:T(8,128)(2,1)} custom-call(s32[1]{0:T(128)} %bitcast.core_ref, f32[1,2048]{1,0:T(1,128)S(1)} %bitcast.50, bf16[288,2048]{1,0:T(8,128)(2,1)S(1)} %get-tuple-element.33.residual_ref, bf16[288,1024]{1,0:T(8,128)(2,1)S(1)} %get-tuple-element.34.values_ref, bf16[16,32,2048]{2,1,0:T(8,128)(2,1)S(1)} %copy-done.1, ...), custom_call_target="tpu_custom_call" | custom-call | flops 4294967296 | bytes 8388608 | tf_op jit(solution)/shard_map/pallas_call | solution.py:446
  149.2 8.0 %all-to-all-start.2 = ((bf16[32,144,128]{2,1,0:T(8,128)(2,1)}), bf16[32,144,128]{2,1,0:T(8,128)(2,1)S(1)}, u32[]{:S(2)}, u32[]{:S(2)}) async-start(bf16[32,144,128]{2,1,0:T(8,128)(2,1)} %shard_map.126), calls=%async_computation.2 | async-start | bytes 2359296 | tf_op jit(solution)/shard_map/all_to_all | solution.py:455
  157.2 5.6 %shard_map.124.attended_ref = bf16[128,2048]{1,0:T(8,128)(2,1)} custom-call(s32[1]{0:T(128)} %bitcast.core_ref, bf16[128,2048]{1,0:T(8,128)(2,1)} %bitcast.58, bf16[128,1024]{1,0:T(8,128)(2,1)} %copy-done.7, bf16[16,176,2048]{2,1,0:T(8,128)(2,1)} %bitcast.55, bf16[16,32,2048]{2,1,0:T(8,128)(2,1)} %copy-done), custom_call_target="tpu_custom_call" | custom-call | flops 536870912 | bytes 6291456 | tf_op jit(solution)/shard_map/pallas_call | solution.py:459
  162.9 55.6 %all-to-all-done.2 = bf16[32,144,128]{2,1,0:T(8,128)(2,1)S(1)} async-done(((bf16[32,144,128]{2,1,0:T(8,128)(2,1)}), bf16[32,144,128]{2,1,0:T(8,128)(2,1)S(1)}, u32[]{:S(2)}, u32[]{:S(2)}) %all-to-all-start.2) | async-done | bytes 1179680 | tf_op jit(solution)/shard_map/all_to_all | solution.py:455
  218.5 2.5 %shard_map.127 = bf16[128,2048]{1,0:T(8,128)(2,1)} custom-call(s32[2,128]{1,0:T(2,128)S(1)} %copy-done.9, f32[2,128]{1,0:T(2,128)S(1)} %bitcast.51, bf16[128,2048]{1,0:T(8,128)(2,1)} %shard_map.124.attended_ref, bf16[4608,128]{1,0:T(8,128)(2,1)S(1)} %bitcast.45), custom_call_target="tpu_custom_call", output_to_operand_aliasing={{}: (2, {})} | custom-call | flops 301989888 | bytes 3145728 | tf_op jit(solution)/shard_map/pallas_call | solution.py:468
  (31 shorter events, 0.1 us)
Async XLA Ops:
  6.5 114.3 %all-gather.4.cloned.1.call-start = ((), (), s32[]{:S(2)}) async-start(), calls=%async_computation.3 | async-start | bytes 12255232 | tf_op jit(solution)/shard_map/all_gather | solution.py:359
  6.5 20.3 %copy-start.12 = (bf16[1,128,576]{1,2,0:T(8,128)(2,1)S(1)}, bf16[1,128,576]{1,2,0:T(8,128)(2,1)}, u32[]{:S(2)}) copy-start(bf16[1,128,576]{1,2,0:T(8,128)(2,1)} %param.14) | copy-start | bytes 442372
  9.9 35.1 %copy-start.4 = (bf16[512,1024]{1,0:T(8,128)(2,1)S(1)}, bf16[512,1024]{1,0:T(8,128)(2,1)}, u32[]{:S(2)}) copy-start(bf16[512,1024]{1,0:T(8,128)(2,1)} %key_up_ref.1) | copy-start | bytes 3145732
  9.9 35.1 %copy-start.6 = (bf16[1,128,1536]{2,1,0:T(8,128)(2,1)S(1)}, bf16[1,128,1536]{2,1,0:T(8,128)(2,1)}, u32[]{:S(2)}) copy-start(bf16[1,128,1536]{2,1,0:T(8,128)(2,1)} %param.13) | copy-start | bytes 1179652
  9.9 78.3 %all-to-all-start = ((bf16[32,144,128]{2,1,0:T(8,128)(2,1)}), bf16[32,144,128]{2,1,0:T(8,128)(2,1)}, u32[]{:S(2)}, u32[]{:S(2)}) async-start(bf16[32,144,128]{2,1,0:T(8,128)(2,1)} %get-tuple-element.22), calls=%async_computation | async-start | bytes 2359296 | tf_op jit(solution)/shard_map/all_to_all | solution.py:360
  39.0 20.3 %collective-permute-start = (bf16[4,576,128]{2,1,0:T(8,128)(2,1)S(1)}, bf16[4,576,128]{2,1,0:T(8,128)(2,1)S(1)}, u32[]{:S(2)}, u32[]{:S(2)}) collective-permute-start(bf16[4,576,128]{2,1,0:T(8,128)(2,1)S(1)} %bitcast.46), channel_id=1, source_target_pairs={{0,128},{32,160},{64,192},{96,224},{128,256},{160,288},{192,320},{... | collective-permute-start | bytes 1769480 | tf_op jit(solution)/shard_map/ppermute | solution.py:367
  42.2 19.3 %collective-permute-start.2 = (bf16[4,576,128]{2,1,0:T(8,128)(2,1)S(1)}, bf16[4,576,128]{2,1,0:T(8,128)(2,1)S(1)}, u32[]{:S(2)}, u32[]{:S(2)}) collective-permute-start(bf16[4,576,128]{2,1,0:T(8,128)(2,1)S(1)} %bitcast.47), channel_id=1, source_target_pairs={{0,384},{32,416},{64,448},{96,480},{128,0},{160,32},{192,64},{224,... | collective-permute-start | bytes 1769480 | tf_op jit(solution)/shard_map/ppermute | solution.py:367
  59.3 14.0 %collective-permute-start.1 = (bf16[2,576,128]{2,1,0:T(8,128)(2,1)S(1)}, bf16[2,576,128]{2,1,0:T(8,128)(2,1)S(1)}, u32[]{:S(2)}, u32[]{:S(2)}) collective-permute-start(bf16[2,576,128]{2,1,0:T(8,128)(2,1)S(1)} %slice.21), channel_id=1, source_target_pairs={{128,256},{160,288},{192,320},{224,352},{256,384},{288,416},{320,4... | collective-permute-start | bytes 884744 | tf_op jit(solution)/shard_map/ppermute | solution.py:367
  61.5 11.9 %collective-permute-start.3 = (bf16[2,576,128]{2,1,0:T(8,128)(2,1)S(1)}, bf16[2,576,128]{2,1,0:T(8,128)(2,1)S(1)}, u32[]{:S(2)}, u32[]{:S(2)}) collective-permute-start(bf16[2,576,128]{2,1,0:T(8,128)(2,1)S(1)} %slice.22), channel_id=1, source_target_pairs={{0,384},{32,416},{64,448},{96,480},{384,256},{416,288},{448,320},{... | collective-permute-start | bytes 884744 | tf_op jit(solution)/shard_map/ppermute | solution.py:367
  68.7 4.6 %copy-start.5 = (bf16[512,1024]{1,0:T(8,128)(2,1)S(1)}, bf16[512,1024]{1,0:T(8,128)(2,1)}, u32[]{:S(2)}) copy-start(bf16[512,1024]{1,0:T(8,128)(2,1)} %value_up_ref.1) | copy-start | bytes 3145732
  68.7 4.6 %copy-start.9 = (s32[2,128]{1,0:T(2,128)S(1)}, s32[2,128]{1,0:T(2,128)}, u32[]{:S(2)}) copy-start(s32[2,128]{1,0:T(2,128)} %get-tuple-element.21.slots_ref) | copy-start | bytes 3076
  78.8 0.7 copy-start.7
  88.2 42.8 %all-to-all-start.1 = ((bf16[32,72,128]{2,1,0:T(8,128)(2,1)}), bf16[32,72,128]{2,1,0:T(8,128)(2,1)S(1)}, u32[]{:S(2)}, u32[]{:S(2)}) async-start(bf16[32,72,128]{2,1,0:T(8,128)(2,1)} %bitcast.36), calls=%async_computation.1 | async-start | bytes 1179648 | tf_op jit(solution)/shard_map/all_to_all | solution.py:422
  123.7 15.9 %collective-permute-start.4 = (bf16[16,32,2048]{2,1,0:T(8,128)(2,1)}, bf16[16,32,2048]{2,1,0:T(8,128)(2,1)S(1)}, u32[]{:S(2)}, u32[]{:S(2)}) collective-permute-start(bf16[16,32,2048]{2,1,0:T(8,128)(2,1)} %shard_map.123.own_ref), channel_id=1, source_target_pairs={{0,1},{1,0},{2,3},{3,2},{4,5},{5,4},{6,7},{7,6},{8,9},{9,8},{10,11... | collective-permute-start | bytes 6291464 | tf_op jit(solution)/shard_map/ppermute | solution.py:436
  131.0 0.9 copy-start.11
  131.8 7.8 %copy-start.1 = (bf16[16,32,2048]{2,1,0:T(8,128)(2,1)S(1)}, bf16[16,32,2048]{2,1,0:T(8,128)(2,1)}, u32[]{:S(2)}) copy-start(bf16[16,32,2048]{2,1,0:T(8,128)(2,1)} %shard_map.123.own_ref) | copy-start | bytes 6291460
  131.8 7.8 %copy-start.8 = (f32[2048]{0:T(1024)S(1)}, f32[2048]{0:T(1024)}, u32[]{:S(2)}) copy-start(f32[2048]{0:T(1024)} %param.18) | copy-start | bytes 24580
  136.3 1.7 copy-start.2
  138.0 1.6 copy-start.3
  139.6 9.6 %copy-start = (bf16[16,32,2048]{2,1,0:T(8,128)(2,1)}, bf16[16,32,2048]{2,1,0:T(8,128)(2,1)S(1)}, u32[]{:S(2)}) copy-start(bf16[16,32,2048]{2,1,0:T(8,128)(2,1)S(1)} %collective-permute-done.4.other_ref) | copy-start | bytes 6291460
  149.2 69.3 %all-to-all-start.2 = ((bf16[32,144,128]{2,1,0:T(8,128)(2,1)}), bf16[32,144,128]{2,1,0:T(8,128)(2,1)S(1)}, u32[]{:S(2)}, u32[]{:S(2)}) async-start(bf16[32,144,128]{2,1,0:T(8,128)(2,1)} %shard_map.126), calls=%async_computation.2 | async-start | bytes 2359296 | tf_op jit(solution)/shard_map/all_to_all | solution.py:455
  157.2 61.3 %copy-start.10 = (f32[1,128,2]{1,2,0:T(2,128)S(1)}, f32[1,128,2]{1,2,0:T(2,128)}, u32[]{:S(2)}) copy-start(f32[1,128,2]{1,2,0:T(2,128)} %param.23) | copy-start | bytes 3076
Sparse Core Ops, SparseCore 0:
  10.4 110.3 all-gather.3
